TPU v7x, 256 devices: a whole 4x4x8 slice. The times are simulated.
256 devices in a mesh: roll: 32 (over y, x, core), tp: 8 (over z).
Axes of the slice: x: 4, y: 4, z: 8, core: 2. Of those that a mesh axis runs over, the one named last changes fastest.
Arguments:
- queries: bfloat16 [4096, 4, 64, 128], P('roll', None, 'tp'), may hold values from -8 to 8
- new_keys: bfloat16 [4096, 4, 8, 128], P('roll', None, 'tp'), may hold values from -6 to 6
- new_values: bfloat16 [4096, 4, 8, 128], P('roll', None, 'tp'), may hold values from -6 to 6
- tail_keys: bfloat16 [4096, 8, 128, 128], P('roll', 'tp'), may hold values from -8 to 8
- tail_values: bfloat16 [4096, 8, 128, 128], P('roll', 'tp'), may hold values from -6 to 6
- prefix_keys: bfloat16 [64, 8, 1024, 128], P('roll', 'tp'), may hold values from -8 to 8
- prefix_values: bfloat16 [64, 8, 1024, 128], P('roll', 'tp'), may hold values from -6 to 6
- route_owner: int32 [32, 128], P('roll', 'tp'), may hold values from 0 to 31, as said below
- group_slot: int32 [32, 128], P('roll', 'tp'), may hold values from 0 to 1
- tail_len: int32 [32, 128], P('roll', 'tp'), may hold values from 1 to 128, 10240 in all within a row
Outputs:
- attended: bfloat16 [4096, 4, 64, 128], P('roll', None, 'tp')
Inputs may be any that keep to these rules, and one draw needn't show every extreme that they name: `route_owner`: within one device's rows each owner is named at most 8 times, and one owner, drawn afresh, is named exactly 8 times by the rows of every device.
All inputs are finite; a program needn't handle non-finite values. No bound on the sum of `tail_len` on one device may be relied on, other than what follows from the above.
Results may differ from a plain program's by a relative error of at most 0.0056.
Values may be sent and summed in bfloat16 or wider, within the bound.
No kernel may reach another device: no remote copies, remote signals or barrier semaphores. Data moves between devices by JAX's collectives and lax.ppermute only.
A program may use at most 192 MiB of HBM per device.

v0:
```python
import math

import jax
import jax.numpy as jnp
from jax import lax
from jax.sharding import PartitionSpec as P


def rounded(values):
    return lax.optimization_barrier(values.astype(jnp.bfloat16)).astype(jnp.float32)


def product(form, left, right):
    return jnp.einsum(
        form, left.astype(jnp.float32), right.astype(jnp.float32), precision=lax.Precision.HIGHEST
    )


def prefix_attention(q_in, slots_in, prefix_keys, prefix_values, scale):
    owners, items, steps, local_heads, width = q_in.shape
    kv_local = prefix_keys.shape[1]
    per_group = local_heads // kv_local
    count = owners * items * steps * per_group
    flat = q_in.reshape(owners * items * steps, kv_local, per_group, width)
    flat = flat.transpose(1, 0, 2, 3).reshape(kv_local, count, width)
    owner_slot = jnp.broadcast_to(
        slots_in[:, :, None, None], (owners, items, steps, per_group)
    ).reshape(-1)
    result = jnp.zeros((kv_local, count, width), jnp.float32)
    log_total = jnp.zeros((kv_local, count), jnp.float32)
    for group in range(prefix_keys.shape[0]):
        scores = product("kqd,kjd->kqj", flat, prefix_keys[group]) * scale
        top = jnp.max(scores, axis=-1, keepdims=True)
        expo = jnp.exp(scores - top)
        total = jnp.sum(expo, axis=-1, keepdims=True)
        partial_value = product("kqj,kjd->kqd", rounded(expo), prefix_values[group]) / total
        picked = (owner_slot == group)[None, :]
        result = jnp.where(picked[..., None], partial_value, result)
        log_total = jnp.where(picked, top[..., 0] + jnp.log(total[..., 0]), log_total)
    result = result.reshape(kv_local, owners, items, steps, per_group, width).transpose(
        1, 2, 3, 0, 4, 5
    )
    log_total = log_total.reshape(kv_local, owners, items, steps, per_group).transpose(
        1, 2, 3, 0, 4
    )
    return (
        result.reshape(owners, items, steps, local_heads, width),
        log_total.reshape(owners, items, steps, local_heads),
    )


def tail_attention(grouped, tail_keys, tail_values, new_keys, new_values, lengths, scale):
    steps = grouped.shape[1]
    slots = tail_keys.shape[2]
    tail_scores = product("rskgd,rktd->rskgt", grouped, tail_keys) * scale
    valid = jnp.arange(slots, dtype=jnp.int32)[None, :] < lengths[:, None]
    tail_scores = jnp.where(valid[:, None, None, None, :], tail_scores, -jnp.inf)
    new_scores = product("rskgd,rukd->rskgu", grouped, new_keys) * scale
    causal = jnp.arange(steps)[None, :] <= jnp.arange(steps)[:, None]
    new_scores = jnp.where(causal[None, :, None, None, :], new_scores, -jnp.inf)
    top = jnp.maximum(
        jnp.max(tail_scores, axis=-1, keepdims=True), jnp.max(new_scores, axis=-1, keepdims=True)
    )
    expo_tail = jnp.exp(tail_scores - top)
    expo_new = jnp.exp(new_scores - top)
    total = jnp.sum(expo_tail, axis=-1, keepdims=True) + jnp.sum(expo_new, axis=-1, keepdims=True)
    summed = product("rskgt,rktd->rskgd", rounded(expo_tail), tail_values)
    summed = summed + product("rskgu,rukd->rskgd", rounded(expo_new), new_values)
    return (summed / total, top[..., 0] + jnp.log(total[..., 0]))


def combine(prefix_out, prefix_lse, tail_out, tail_lse):
    upper = jnp.maximum(prefix_lse, tail_lse)
    weight_p = jnp.exp(prefix_lse - upper)
    weight_t = jnp.exp(tail_lse - upper)
    return (weight_p[..., None] * prefix_out + weight_t[..., None] * tail_out) / (
        weight_p + weight_t
    )[..., None]


def body(
    queries,
    new_keys,
    new_values,
    tail_keys,
    tail_values,
    prefix_keys,
    prefix_values,
    route_owner,
    group_slot,
    tail_len,
):
    owner_all, slot_all, length_all = (
        lax.all_gather(route_owner, "tp", axis=1, tiled=True),
        lax.all_gather(group_slot, "tp", axis=1, tiled=True),
        lax.all_gather(tail_len, "tp", axis=1, tiled=True),
    )
    owner_rows = owner_all.reshape(-1)
    slot_rows = slot_all.reshape(-1)
    length_rows = length_all.reshape(-1)
    rows, steps, local_heads, width = queries.shape
    owners = lax.axis_size("roll")
    capacity = 2 * rows // owners
    scale = 1.0 / math.sqrt(width)
    kv_local = prefix_keys.shape[1]
    grouped = queries.reshape(rows, steps, kv_local, local_heads // kv_local, width)
    out_t, lse_t = tail_attention(
        grouped, tail_keys, tail_values, new_keys, new_values, length_rows, scale
    )
    tail_out = out_t.reshape(rows, steps, local_heads, width)
    tail_lse = lse_t.reshape(rows, steps, local_heads)
    onehot = (owner_rows[:, None] == jnp.arange(owners, dtype=jnp.int32)[None, :]).astype(jnp.int32)
    before = jnp.cumsum(onehot, axis=0) - onehot
    rank = jnp.sum(before * onehot, axis=1)
    position = owner_rows * capacity + rank
    placed = position[None, :] == jnp.arange(owners * capacity, dtype=jnp.int32)[:, None]
    dispatch = placed.astype(jnp.bfloat16)
    dispatch_wide = placed.astype(jnp.float32)
    sent_queries = jnp.dot(dispatch, queries.reshape(rows, -1), preferred_element_type=jnp.float32)
    sent_queries = sent_queries.astype(jnp.bfloat16).reshape(
        owners, capacity, steps, local_heads, width
    )
    sent_slots = (jnp.sum(jnp.where(placed, slot_rows[None, :] + 1, 0), axis=1) - 1).reshape(
        owners, capacity
    )
    q_in = lax.all_to_all(sent_queries, "roll", split_axis=0, concat_axis=0, tiled=True)
    slots_in = lax.all_to_all(sent_slots, "roll", split_axis=0, concat_axis=0, tiled=True)
    prefix_out, prefix_lse = prefix_attention(q_in, slots_in, prefix_keys, prefix_values, scale)
    out_back = lax.all_to_all(
        prefix_out.astype(jnp.bfloat16), "roll", split_axis=0, concat_axis=0, tiled=True
    )
    lse_back = lax.all_to_all(prefix_lse, "roll", split_axis=0, concat_axis=0, tiled=True)
    prefix_rows = jnp.dot(
        dispatch_wide.T,
        out_back.reshape(owners * capacity, -1).astype(jnp.float32),
        precision=lax.Precision.HIGHEST,
    )
    lse_rows = jnp.dot(
        dispatch_wide.T, lse_back.reshape(owners * capacity, -1), precision=lax.Precision.HIGHEST
    )
    merged = combine(
        prefix_rows.reshape(rows, steps, local_heads, width),
        lse_rows.reshape(rows, steps, local_heads),
        tail_out,
        tail_lse,
    )
    return merged.astype(jnp.bfloat16)


def solution(mesh):
    return jax.shard_map(
        body,
        mesh=mesh,
        in_specs=(
            P("roll", None, "tp", None),
            P("roll", None, "tp", None),
            P("roll", None, "tp", None),
            P("roll", "tp", None, None),
            P("roll", "tp", None, None),
            P("roll", "tp", None, None),
            P("roll", "tp", None, None),
            P("roll", "tp"),
            P("roll", "tp"),
            P("roll", "tp"),
        ),
        out_specs=P("roll", None, "tp", None),
        check_vma=False,
    )
```

profile of v0, /device:TPU:1, one launch (start us, length us, event | category | flops | bytes accessed | tf_op | source)
XLA Modules:
  0.0 213.7 jit_solution(5798142219360827742)
XLA Ops:
  0.0 1.3 dynamic-slice
  2.0 0.8 bitcast_dynamic-update-slice_fusion.2
  2.7 0.7 bitcast_dynamic-update-slice_fusion
  3.5 0.7 bitcast_dynamic-update-slice_fusion.1
  4.2 14.6 %all-reduce.3 = (s32[128]{0:T(128)}, s32[128]{0:T(128)S(1)}, s32[128]{0:T(128)S(1)}) all-reduce(s32[128]{0:T(128)S(1)} %bitcast_dynamic-update-slice_fusion, s32[128]{0:T(128)S(1)} %bitcast_dynamic-update-slice_fusion.2, s32[128]{0:T(128)S(1)} %bitcast_dynamic-update-slice_fusion.1), channel_id=1, replica_groups=mesh['roll'=32,'tp'=8] {'tp'}, use_global_device_ids=true, to_apply=%add.2 | all-reduce | flops 384 | bytes 3072
  18.8 0.1 fusion.64
  18.9 0.2 reduce_window_sum.11
  19.0 0.2 select_reduce_fusion.1
  19.2 0.1 select_reduce_fusion
  19.3 0.7 sub.51
  20.0 10.6 %all-to-all-start = ((s32[32,1,8]{2,1,0:T(1,128)}), s32[32,1,8]{2,1,0:T(1,128)S(1)}, u32[]{:S(2)}, u32[]{:S(2)}) async-start(s32[32,1,8]{2,1,0:T(1,128)} %bitcast.4), calls=%async_computation | async-start | bytes 32768 | tf_op jit(solution)/shard_map/all_to_all | solution.py:127
  30.7 2.1 convolution_convert_fusion
  32.8 1.8 copy.44
  34.6 3.0 %all-to-all-done = s32[32,1,8]{2,1,0:T(1,128)S(1)} async-done(((s32[32,1,8]{2,1,0:T(1,128)}), s32[32,1,8]{2,1,0:T(1,128)S(1)}, u32[]{:S(2)}, u32[]{:S(2)}) %all-to-all-start) | async-done | bytes 1056 | tf_op jit(solution)/shard_map/all_to_all | solution.py:127
  37.6 4.6 %all-to-all-start.1 = ((bf16[32,8,4,8,128]{4,3,2,1,0:T(8,128)(2,1)}), bf16[32,8,4,8,128]{4,3,2,1,0:T(8,128)(2,1)S(1)}, u32[]{:S(2)}, u32[]{:S(2)}) async-start(bf16[32,8,4,8,128]{4,3,2,1,0:T(8,128)(2,1)} %copy.44), calls=%async_computation.1 | async-start | bytes 4194304 | tf_op jit(solution)/shard_map/all_to_all | solution.py:126
  42.2 6.5 %fusion.71 = (f32[128,4,8]{2,1,0:T(4,128)}, f32[128,4,1,8,4]{3,4,1,0,2:T(4,128)}) fusion(bf16[128,4,8,128]{3,2,1,0:T(8,128)(2,1)S(1)} %copy-done.1, bf16[128,4,1,128]{3,1,2,0:T(4,128)(2,1)S(1)} %copy-done.13, pred[4,4]{1,0:T(4,128)(4,1)S(1)} %iota_compare_fusion.4), kind=kOutput, calls=%fused_computation.90 | convolution fusion | flops 4239360 | bytes 1261584 | tf_op jit(solution)/shard_map/rskgd,rukd->rskgu/dot_general | solution.py:14
  48.6 0.1 copy.42
  48.7 0.1 copy.43
  48.8 0.1 copy.46
  48.9 0.3 broadcast_in_dim.90
  49.3 0.3 eq.87
  49.5 0.3 broadcast_in_dim.89
  49.9 0.3 eq.86
  50.1 19.8 %all-to-all-done.1 = bf16[32,8,4,8,128]{4,3,2,1,0:T(8,128)(2,1)S(1)} async-done(((bf16[32,8,4,8,128]{4,3,2,1,0:T(8,128)(2,1)}), bf16[32,8,4,8,128]{4,3,2,1,0:T(8,128)(2,1)S(1)}, u32[]{:S(2)}, u32[]{:S(2)}) %all-to-all-start.1) | async-done | bytes 2097184 | tf_op jit(solution)/shard_map/all_to_all | solution.py:126
  69.9 14.0 %multiply_reduce_fusion = (f32[8192]{0:T(1024)S(1)}, f32[8192,1024]{0,1:T(8,128)}) fusion(bf16[8192,128]{1,0:T(8,128)(2,1)S(1)} %bitcast.158, bf16[2,1,1024,128]{3,2,1,0:T(8,128)(2,1)} %param.15), kind=kOutput, calls=%fused_computation.2 | convolution fusion | flops 2164252672 | bytes 35946496 | tf_op jit(solution)/shard_map/kqd,kjd->kqj/dot_general | solution.py:14
  84.0 13.0 %multiply_reduce_fusion.1 = (f32[8192]{0:T(1024)S(1)}, f32[8192,1024]{0,1:T(8,128)}) fusion(bf16[8192,128]{1,0:T(8,128)(2,1)S(1)} %bitcast.159, bf16[2,1,1024,128]{3,2,1,0:T(8,128)(2,1)S(1)} %copy-done.3), kind=kOutput, calls=%fused_computation.3 | convolution fusion | flops 2164252672 | bytes 35946496 | tf_op jit(solution)/shard_map/kqd,kjd->kqj/dot_general | solution.py:14
  97.0 19.1 %fusion.3 = (f32[8192]{0:T(1024)S(1)}, bf16[1,8192,1024]{1,2,0:T(8,128)(2,1)}) fusion(f32[8192,1024]{0,1:T(8,128)} %get-tuple-element.27, f32[8192]{0:T(1024)S(1)} %get-tuple-element.26), kind=kLoop, calls=%fused_computation.7 | loop fusion | flops 33546240 | bytes 50397184 | tf_op jit(solution)/shard_map/reduce_sum | solution.py:35
  116.2 0.6 add.77
  116.8 19.2 %fusion.1 = (f32[8192]{0:T(1024)S(1)}, bf16[1,8192,1024]{1,2,0:T(8,128)(2,1)}) fusion(f32[8192,1024]{0,1:T(8,128)} %get-tuple-element.29, f32[8192]{0:T(1024)S(1)} %get-tuple-element.28), kind=kLoop, calls=%fused_computation.5 | loop fusion | flops 33546240 | bytes 50397184 | tf_op jit(solution)/shard_map/reduce_sum | solution.py:35
  136.0 0.6 add.75
  136.7 0.9 select_select_fusion
  137.6 1.1 reshape.323
  138.7 5.9 %all-to-all-start.2 = ((f32[32,1,256]{2,1,0:T(1,128)}), f32[32,1,256]{2,1,0:T(1,128)S(1)}, u32[]{:S(2)}, u32[]{:S(2)}) async-start(f32[32,1,256]{2,1,0:T(1,128)} %reshape.323), calls=%async_computation.2 | async-start | bytes 65536 | tf_op jit(solution)/shard_map/all_to_all | solution.py:132
  144.7 0.0 copy-start.12
  144.7 9.8 %fusion.22 = bf16[8192,128]{1,0:T(8,128)(2,1)S(1)} fusion(bf16[1,8192,1024]{1,2,0:T(8,128)(2,1)} %get-tuple-element.15, f32[8192]{0:T(1024)S(1)} %get-tuple-element.14, pred[8192]{0:T(1024)(128)(4,1)S(1)} %eq.87, bf16[2,1,1024,128]{3,2,1,0:T(8,128)(2,1)} %param.16), kind=kOutput, calls=%fused_computation.18 | convolution fusion | flops 2149580800 | bytes 19177472 | tf_op jit(solution)/shard_map/kqj,kjd->kqd/dot_general | solution.py:14
  154.5 10.7 %fusion.16 = bf16[8192,128]{1,0:T(8,128)(2,1)} fusion(bf16[8192,128]{1,0:T(8,128)(2,1)S(1)} %fusion.22, bf16[1,8192,1024]{1,2,0:T(8,128)(2,1)} %get-tuple-element.13, f32[8192]{0:T(1024)S(1)} %get-tuple-element.12, pred[8192]{0:T(1024)(128)(4,1)S(1)} %eq.86, bf16[2,1,1024,128]{3,2,1,0:T(8,128)(2,1)S(1)} %copy-done.12), kind=kOutput, calls=%fused_computation.16 | convolution fusion | flops 2149580800 | bytes 21274624 | tf_op jit(solution)/shard_map/kqj,kjd->kqd/dot_general | solution.py:14
  165.2 0.0 all-to-all-done.2
  165.2 0.6 copy-done.7
  165.8 7.5 %all-to-all-start.3 = ((bf16[32,8,4,8,128]{4,3,2,1,0:T(8,128)(2,1)}), bf16[32,8,4,8,128]{4,3,2,1,0:T(8,128)(2,1)S(1)}, u32[]{:S(2)}, u32[]{:S(2)}) async-start(bf16[32,8,4,8,128]{4,3,2,1,0:T(8,128)(2,1)} %bitcast.162), calls=%async_computation.3 | async-start | bytes 4194304 | tf_op jit(solution)/shard_map/all_to_all | solution.py:129
  173.3 0.7 iota_compare_fusion.2
  174.0 0.7 copy.50
  174.7 5.8 %bitcast_reduce_fusion = (f32[128,4,8]{2,1,0:T(4,128)S(1)}, f32[128,128,4,8]{1,3,2,0:T(8,128)}) fusion(pred[128,128]{1,0:T(8,128)(4,1)S(1)} %iota_compare_fusion.2, bf16[128,4,8,128]{3,2,1,0:T(8,128)(2,1)S(1)} %copy-done.1, bf16[128,1,128,128]{3,2,1,0:T(8,128)(2,1)} %param.13), kind=kOutput, calls=%fused_computation.30 | convolution fusion | flops 135786496 | bytes 7372800 | tf_op jit(solution)/shard_map/rskgd,rktd->rskgt/dot_general | solution.py:14
  180.6 0.1 copy.49
  180.7 0.8 max.14
  181.4 0.1 copy.51
  181.6 0.4 copy-done.5
  182.0 2.6 %fusion.41 = (f32[128,4,8]{2,1,0:T(4,128)S(1)}, bf16[128,4,1,8,4]{3,4,1,0,2:T(4,128)(2,1)}) fusion(f32[128,4,1,8,4]{3,4,1,0,2:T(4,128)} %get-tuple-element.25, f32[128,4,8]{2,1,0:T(4,128)S(1)} %copy.51), kind=kLoop, calls=%fused_computation.44 | loop fusion | flops 45056 | bytes 131072 | tf_op jit(solution)/shard_map/reduce_sum | solution.py:66
  184.6 0.7 copy.54
  185.3 3.3 %fusion.34 = (f32[128,4,8]{2,1,0:T(4,128)}, bf16[128,4,1,8,128]{4,3,1,0,2:T(8,128)(2,1)S(1)}) fusion(f32[128,128,4,8]{1,3,2,0:T(8,128)} %get-tuple-element.23, f32[128,4,8]{2,1,0:T(4,128)S(1)} %copy.51, pred[128,128]{1,0:T(8,128)(4,1)S(1)} %iota_compare_fusion.2), kind=kLoop, calls=%fused_computation.35 | loop fusion | flops 2617344 | bytes 3194880 | tf_op jit(solution)/shard_map/reduce_sum | solution.py:66
  188.7 1.0 copy.53
  189.7 2.9 %fusion.42 = f32[128,4,8,128]{3,2,1,0:T(8,128)} fusion(bf16[128,4,1,8,4]{3,4,1,0,2:T(4,128)(2,1)} %get-tuple-element.19, bf16[128,4,1,128]{3,1,2,0:T(4,128)(2,1)S(1)} %copy-done), kind=kOutput, calls=%fused_computation.45 | convolution fusion | flops 4194304 | bytes 2260992 | tf_op jit(solution)/shard_map/rskgu,rukd->rskgd/dot_general | solution.py:14
  192.6 4.8 %fusion.25 = f32[128,4,8,128]{3,2,1,0:T(8,128)} fusion(bf16[128,1,128,128]{3,2,1,0:T(8,128)(2,1)} %param.14, bf16[128,4,1,8,128]{4,3,1,0,2:T(8,128)(2,1)S(1)} %get-tuple-element.17), kind=kOutput, calls=%fused_computation.20 | convolution fusion | flops 134217728 | bytes 7340032 | tf_op jit(solution)/shard_map/rskgt,rktd->rskgd/dot_general | solution.py:14
  197.3 0.5 broadcast.131
  197.9 0.7 reduce.12
  198.6 0.7 reshape.324
  199.2 0.3 reshape.322
  199.5 0.1 copy.66
  199.6 0.0 copy-done.9
  199.6 0.3 fusion.68
  199.9 1.3 all-to-all-done.3
  201.2 2.3 %reshape.286 = bf16[256,4096]{1,0:T(8,128)(2,1)} reshape(bf16[32,8,4,8,128]{4,3,2,1,0:T(8,128)(2,1)S(1)} %all-to-all-done.3) | data formatting | bytes 4194304 | tf_op jit(solution)/shard_map/reshape | solution.py:135
  203.5 4.3 %copy.55 = bf16[256,4096]{0,1:T(8,128)(2,1)} copy(bf16[256,4096]{1,0:T(8,128)(2,1)} %reshape.286) | data formatting | bytes 4194304 | tf_op jit(solution)/shard_map/reshape | solution.py:135
  207.7 4.3 %fusion.31 = bf16[128,4,8,128]{3,0,2,1:T(8,128)(2,1)S(1)} fusion(f32[128,4,8,128]{3,2,1,0:T(8,128)} %fusion.42, f32[128,4,8,128]{3,2,1,0:T(8,128)S(1)} %copy-done.2, bf16[4,8,128,256]{3,2,1,0:T(8,128)(2,1)} %bitcast.163, f32[128,4,8]{0,2,1:T(8,128)S(1)} %get-tuple-element.8, f32[128,4,8]{0,2,1:T(8,128)S(1)} %get-tuple-element.11, ...), kind=kOutput, calls=%fused_computation.27 | convolution fusion | flops 272138240 | bytes 7406080 | tf_op jit(solution)/shard_map/dot_general | solution.py:133
  212.1 1.6 copy.58
  (33 shorter events, 0.1 us)
Async XLA Ops:
  0.0 189.7 %copy-start = (bf16[128,4,1,128]{3,1,2,0:T(4,128)(2,1)S(1)}, bf16[128,4,1,128]{3,1,2,0:T(4,128)(2,1)}, u32[]{:S(2)}) copy-start(bf16[128,4,1,128]{3,1,2,0:T(4,128)(2,1)} %param.12) | copy-start | bytes 393220
  19.2 15.4 %copy-start.10 = (s32[128]{0:T(128)}, s32[128]{0:T(128)S(1)}, u32[]{:S(2)}) copy-start(s32[128]{0:T(128)S(1)} %get-tuple-element.30) | copy-start | bytes 1540
  20.0 17.5 %all-to-all-start = ((s32[32,1,8]{2,1,0:T(1,128)}), s32[32,1,8]{2,1,0:T(1,128)S(1)}, u32[]{:S(2)}, u32[]{:S(2)}) async-start(s32[32,1,8]{2,1,0:T(1,128)} %bitcast.4), calls=%async_computation | async-start | bytes 32768 | tf_op jit(solution)/shard_map/all_to_all | solution.py:127
  34.6 7.6 %copy-start.1 = (bf16[128,4,8,128]{3,2,1,0:T(8,128)(2,1)S(1)}, bf16[128,4,8,128]{3,2,1,0:T(8,128)(2,1)}, u32[]{:S(2)}) copy-start(bf16[128,4,8,128]{3,2,1,0:T(8,128)(2,1)} %param.10) | copy-start | bytes 3145732
  34.6 7.6 %copy-start.13 = (bf16[128,4,1,128]{3,1,2,0:T(4,128)(2,1)S(1)}, bf16[128,4,1,128]{3,1,2,0:T(4,128)(2,1)}, u32[]{:S(2)}) copy-start(bf16[128,4,1,128]{3,1,2,0:T(4,128)(2,1)} %param.11) | copy-start | bytes 393220
  37.6 32.4 %all-to-all-start.1 = ((bf16[32,8,4,8,128]{4,3,2,1,0:T(8,128)(2,1)}), bf16[32,8,4,8,128]{4,3,2,1,0:T(8,128)(2,1)S(1)}, u32[]{:S(2)}, u32[]{:S(2)}) async-start(bf16[32,8,4,8,128]{4,3,2,1,0:T(8,128)(2,1)} %copy.44), calls=%async_computation.1 | async-start | bytes 4194304 | tf_op jit(solution)/shard_map/all_to_all | solution.py:126
  69.9 14.0 %copy-start.3 = (bf16[2,1,1024,128]{3,2,1,0:T(8,128)(2,1)S(1)}, bf16[2,1,1024,128]{3,2,1,0:T(8,128)(2,1)}, u32[]{:S(2)}) copy-start(bf16[2,1,1024,128]{3,2,1,0:T(8,128)(2,1)} %param.15) | copy-start | bytes 1572868
  138.7 26.5 %all-to-all-start.2 = ((f32[32,1,256]{2,1,0:T(1,128)}), f32[32,1,256]{2,1,0:T(1,128)S(1)}, u32[]{:S(2)}, u32[]{:S(2)}) async-start(f32[32,1,256]{2,1,0:T(1,128)} %reshape.323), calls=%async_computation.2 | async-start | bytes 65536 | tf_op jit(solution)/shard_map/all_to_all | solution.py:132
  144.7 9.8 %copy-start.12 = (bf16[2,1,1024,128]{3,2,1,0:T(8,128)(2,1)S(1)}, bf16[2,1,1024,128]{3,2,1,0:T(8,128)(2,1)}, u32[]{:S(2)}) copy-start(bf16[2,1,1024,128]{3,2,1,0:T(8,128)(2,1)} %param.16) | copy-start | bytes 1572868
  165.2 0.6 copy-start.7
  165.2 8.8 %copy-start.4 = (f32[128,4,8]{2,1,0:T(4,128)S(1)}, f32[128,4,8]{2,1,0:T(4,128)}, u32[]{:S(2)}) copy-start(f32[128,4,8]{2,1,0:T(4,128)} %get-tuple-element.24) | copy-start | bytes 49156
  165.8 35.3 %all-to-all-start.3 = ((bf16[32,8,4,8,128]{4,3,2,1,0:T(8,128)(2,1)}), bf16[32,8,4,8,128]{4,3,2,1,0:T(8,128)(2,1)S(1)}, u32[]{:S(2)}, u32[]{:S(2)}) async-start(bf16[32,8,4,8,128]{4,3,2,1,0:T(8,128)(2,1)} %bitcast.162), calls=%async_computation.3 | async-start | bytes 4194304 | tf_op jit(solution)/shard_map/all_to_all | solution.py:129
  181.4 0.6 copy-start.5
  192.6 5.3 %copy-start.8 = (f32[32,1,256]{2,1,0:T(1,128)S(1)}, f32[32,1,256]{2,1,0:T(1,128)}, u32[]{:S(2)}) copy-start(f32[32,1,256]{2,1,0:T(1,128)} %copy-done.7) | copy-start | bytes 98308
  192.6 7.0 %copy-start.6 = (f32[128,4,8]{0,2,1:T(8,128)S(1)}, f32[128,4,8]{0,2,1:T(8,128)}, u32[]{:S(2)}) copy-start(f32[128,4,8]{0,2,1:T(8,128)} %copy-done.5) | copy-start | bytes 49156
  192.6 7.0 %copy-start.9 = (f32[128,4,8]{0,2,1:T(8,128)S(1)}, f32[128,4,8]{0,2,1:T(8,128)}, u32[]{:S(2)}) copy-start(f32[128,4,8]{0,2,1:T(8,128)} %copy.54) | copy-start | bytes 49156
  192.6 7.0 %copy-start.11 = (s32[128]{0:T(128)S(1)}, s32[128]{0:T(128)}, u32[]{:S(2)}) copy-start(s32[128]{0:T(128)} %copy-done.10) | copy-start | bytes 1540
  203.5 4.3 %copy-start.2 = (f32[128,4,8,128]{3,2,1,0:T(8,128)S(1)}, f32[128,4,8,128]{3,2,1,0:T(8,128)}, u32[]{:S(2)}) copy-start(f32[128,4,8,128]{3,2,1,0:T(8,128)} %fusion.25) | copy-start | bytes 6291460
where the time goes:
time: 215 us; the launch traced here: 214 us
  matrix products  74.2 us (35%)
  other arithmetic  47.9 us (22%)
  starting transfers between devices  28.7 us (13%)
  waiting for transfers between devices  24 us (11%)
  local copies, waits for them, and re-layouts  23.4 us (11%)
  blocking collectives  14.6 us (7%)
    dot_general x8, matrix products, product(): jnp.einsum(form, left.astype(jnp.float32), right.astype(jnp.float32), pre...  67.5 us
    reduce_sum x2, other arithmetic, prefix_attention(): total = jnp.sum(expo, axis=-1, keepdims=True)  38.3 us
    all_to_all x1, waiting for transfers between devices, body(): lax.all_to_all(sent_queries, 'roll', split_axis=0, concat_axis=0, tiled=T...  19.8 us
    unnamed x1, blocking collectives  14.6 us
    all_to_all x1, starting transfers between devices, body(): lax.all_to_all(sent_slots, 'roll', split_axis=0, concat_axis=0, tiled=True)  10.6 us
    all_to_all x1, starting transfers between devices, body(): lax.all_to_all(prefix_out.astype(jnp.bfloat16), 'roll', split_axis=0, con...  7.49 us
    reshape x2, local copies, waits for them, and re-layouts, body(): out_back.reshape(owners * capacity, -1).astype(jnp.float32)  6.57 us
    unnamed x37, local copies, waits for them, and re-layouts  6.42 us
  transfers between devices with their start and end apart: 4, of which 3 were waited for; matrix products, arithmetic and copies ran while one was open for 27% of the time, Pallas kernels for 0%

commit v1 on v0

v1 whole, which is shorter than its diff:
```python
import functools
import math

import jax
import jax.numpy as jnp
from jax import lax
from jax.experimental import pallas as pl
from jax.experimental.pallas import tpu as pltpu
from jax.sharding import PartitionSpec as P

LOG2E = math.log2(math.e)
MIB = 1 << 20
F32 = jnp.float32
BF16 = jnp.bfloat16
EXTRA = 16


def lane_group_mask(per_row, width):
    sub = lax.broadcasted_iota(jnp.int32, (per_row, width), 0)
    lane = lax.broadcasted_iota(jnp.int32, (per_row, width), 1)
    return (lane % per_row) == sub


def pack_kernel(cap, per_row, code_ref, q_ref, out_ref, place_ref, count_ref):
    owners = count_ref.shape[0] // 2
    rows = place_ref.shape[0]
    block = cap * per_row + EXTRA
    line = code_ref.shape[1]
    for i in range(2 * owners):
        count_ref[i] = 0

    def clear(i, carry):
        out_ref[pl.ds(pl.multiple_of(i * block, EXTRA), block), :] = jnp.zeros((block, 128), BF16)
        return carry

    lax.fori_loop(0, owners, clear, 0)

    def one(r, carry):
        group = lax.shift_right_logical(code_ref[r // line, r % line], 8)
        taken = count_ref[group]
        count_ref[group] = taken + 1
        owner = lax.shift_right_logical(group, 1)
        slot = jnp.where((group & 1) == 1, cap - 1 - taken, taken)
        place_ref[r] = owner * cap + slot
        start = pl.multiple_of(owner * block + slot * per_row, 16)
        out_ref[pl.ds(start, per_row), :] = q_ref[pl.ds(pl.multiple_of(r * per_row, per_row), per_row), :]
        return carry

    lax.fori_loop(0, rows, one, 0, unroll=8)
    lane = lax.broadcasted_iota(jnp.int32, (EXTRA, 128), 1)
    for o in range(owners):
        first = count_ref[2 * o].astype(F32)
        second = count_ref[2 * o + 1].astype(F32)
        out_ref[o * block + cap * per_row:(o + 1) * block, :] = jnp.where(lane < 64, first, second).astype(BF16)


def tail_kernel(steps, per_row, batch, scale, code_ref, q_ref, tk_ref, tv_ref, nk_ref, nv_ref, out_ref, lse_ref):
    base = pl.program_id(0) * batch
    line = code_ref.shape[1]
    slots = tk_ref.shape[0] // batch
    heads = per_row // steps
    total_rows = batch * per_row
    q = q_ref[...]
    parts = []
    lane = lax.broadcasted_iota(jnp.int32, (per_row, slots), 1)
    for i in range(batch):
        r = base + i
        length = code_ref[r // line, r % line] & 255
        s = lax.dot_general(
            q[i * per_row:(i + 1) * per_row], tk_ref[i * slots:(i + 1) * slots, :],
            (((1,), (1,)), ((), ())), preferred_element_type=F32,
        )
        parts.append(jnp.where(lane < length, s, -jnp.inf))
    st = jnp.concatenate(parts, axis=0)
    sn = lax.dot_general(q, nk_ref[...], (((1,), (1,)), ((), ())), preferred_element_type=F32)
    row = lax.broadcasted_iota(jnp.int32, sn.shape, 0)
    col = lax.broadcasted_iota(jnp.int32, sn.shape, 1)
    own = (row // per_row) == (col // steps)
    causal = (col % steps) <= ((row % per_row) // heads)
    sn = jnp.where(own & causal, sn, -jnp.inf)
    top = jnp.maximum(jnp.max(st, axis=1, keepdims=True), jnp.max(sn, axis=1, keepdims=True))
    et = jnp.exp2((st - top) * (scale * LOG2E))
    en = jnp.exp2((sn - top) * (scale * LOG2E))
    total = jnp.sum(et, axis=1, keepdims=True) + jnp.sum(en, axis=1, keepdims=True)
    pt = et.astype(BF16)
    summed = jnp.concatenate(
        [
            jnp.dot(pt[i * per_row:(i + 1) * per_row], tv_ref[i * slots:(i + 1) * slots, :], preferred_element_type=F32)
            for i in range(batch)
        ],
        axis=0,
    )
    summed = summed + jnp.dot(en.astype(BF16), nv_ref[...], preferred_element_type=F32)
    out_ref[...] = summed / total
    lse = top * scale + jnp.log(total)
    mask = lane_group_mask(per_row, 128)
    for i in range(batch):
        one = jnp.where(mask, lse[i * per_row:(i + 1) * per_row], 0.0)
        lse_ref[i:i + 1, :] = jnp.sum(one, axis=0, keepdims=True)


def prefix_kernel(cap, per_row, pref, scale, x_ref, k_ref, v_ref, out_ref, wide_ref, meta_ref, lse_ref, count_ref, list_ref, sem):
    block = cap * per_row + EXTRA
    sources = x_ref.shape[0] // block
    data = cap * per_row
    lane = lax.broadcasted_iota(jnp.int32, (1, 128), 1)
    for s in range(sources):
        tile = x_ref[s * block + data:(s + 1) * block, :].astype(F32)
        meta_ref[s:s + 1, :] = tile[0:1, :].astype(jnp.int32)
    copy = pltpu.make_async_copy(meta_ref, count_ref, sem)
    copy.start()
    groups = v_ref.shape[0] // pref
    wide_ref[:, 0:128] = v_ref[...]
    wide_ref[:, 128:256] = jnp.ones((groups * pref, 128), BF16)
    lse_ref[...] = jnp.zeros(lse_ref.shape, F32)
    copy.wait()
    found = []
    for g in range(2):
        at = jnp.int32(0)
        for s in range(sources):
            for i in range(cap):
                list_ref[g, at + i] = s * cap + (i if g == 0 else cap - 1 - i)
            at = at + count_ref[s, 64 * g]
        found.append(at)
        last = list_ref[g, jnp.maximum(at - 1, 0)]
        for i in range(cap):
            list_ref[g, at + i] = last
    first_blocks = (found[0] + 7) // 8
    blocks = first_blocks + (found[1] + 7) // 8
    mask = lane_group_mask(per_row, 128)

    def one(b, carry):
        g = (b >= first_blocks).astype(jnp.int32)
        j = (b - g * first_blocks) * 8
        slots = [list_ref[g, j + i] for i in range(8)]
        starts = [pl.multiple_of((s // cap) * block + (s % cap) * per_row, 16) for s in slots]
        q = jnp.concatenate([x_ref[pl.ds(a, per_row), :] for a in starts], axis=0)
        here = pl.multiple_of(g * pref, pref)
        score = lax.dot_general(
            q, k_ref[pl.ds(here, pref), :], (((1,), (1,)), ((), ())), preferred_element_type=F32
        )
        top = jnp.max(score, axis=1, keepdims=True)
        expo = jnp.exp2((score - top) * (scale * LOG2E)).astype(BF16)
        both = jnp.dot(expo, wide_ref[pl.ds(here, pref), :], preferred_element_type=F32)
        total = both[:, 128:256]
        result = (both[:, 0:128] / total).astype(BF16)
        lse = top * scale + jnp.log(total)
        for i in range(8):
            part = slice(i * per_row, (i + 1) * per_row)
            out_ref[pl.ds(starts[i], per_row), :] = result[part]
            lse_ref[pl.ds(slots[i], 1), :] = jnp.sum(jnp.where(mask, lse[part], 0.0), axis=0, keepdims=True)
        return carry

    lax.fori_loop(0, blocks, one, 0)
    for s in range(sources):
        full = lse_ref[s * cap:(s + 1) * cap, :]
        high = full.astype(BF16).astype(F32)
        rest = full - high
        mid = rest.astype(BF16).astype(F32)
        low = rest - mid
        lanes = lax.broadcasted_iota(jnp.int32, full.shape, 1)
        sent = jnp.where(lanes < per_row, high, jnp.where(lanes < 2 * per_row, mid, low))
        sent = jnp.concatenate([sent, jnp.zeros((EXTRA - cap, 128), F32)], axis=0)
        out_ref[s * block + data:(s + 1) * block, :] = sent.astype(BF16)


def merge_kernel(cap, per_row, batch, place_ref, x_ref, tail_ref, lse_ref, out_ref, sent_ref):
    block = cap * per_row + EXTRA
    owners = x_ref.shape[0] // block
    step = pl.program_id(0)

    @pl.when(step == 0)
    def _():
        for o in range(owners):
            tile = x_ref[o * block + cap * per_row:(o + 1) * block, :].astype(F32)
            sent_ref[o * cap:(o + 1) * cap, :] = tile[0:cap, :]

    mask = lane_group_mask(per_row, 128)
    lane = lax.broadcasted_iota(jnp.int32, (1, 128), 1)

    def one(i, carry):
        place = place_ref[step * batch + i]
        start = pl.multiple_of((place // cap) * block + (place % cap) * per_row, 16)
        terms = jnp.where(lane < 3 * per_row, sent_ref[pl.ds(place, 1), :], -lse_ref[pl.ds(i, 1), :])
        ahead = jnp.sum(jnp.where(mask, terms, 0.0), axis=1, keepdims=True)
        prefix = x_ref[pl.ds(start, per_row), :].astype(F32)
        here = pl.ds(pl.multiple_of(i * per_row, per_row), per_row)
        weight_p = 1.0 / (1.0 + jnp.exp(-ahead))
        weight_t = 1.0 / (1.0 + jnp.exp(ahead))
        out_ref[here, :] = (weight_p * prefix + weight_t * tail_ref[here, :]).astype(BF16)
        return carry

    lax.fori_loop(0, batch, one, 0, unroll=8)


def vmem():
    return pl.BlockSpec(memory_space=pltpu.VMEM)


def smem():
    return pl.BlockSpec(memory_space=pltpu.SMEM)


def body(
    queries, new_keys, new_values, tail_keys, tail_values, prefix_keys, prefix_values, route_owner, group_slot, tail_len
):
    rows, steps, heads, width = queries.shape
    owners = lax.axis_size("roll")
    cap = 8
    per_row = steps * heads
    scale = 1.0 / math.sqrt(width)
    slots = tail_keys.shape[2]
    pref = prefix_keys.shape[2]
    groups = prefix_keys.shape[0]
    block = cap * per_row + EXTRA
    code = (route_owner * 2 + group_slot) * 256 + tail_len
    codes = lax.all_gather(code, "tp", axis=0, tiled=True)
    flat = queries.reshape(rows * per_row, width)
    params = functools.partial(pltpu.CompilerParams, vmem_limit_bytes=32 * MIB)

    sent, place = pl.pallas_call(
        functools.partial(pack_kernel, cap, per_row),
        out_shape=(
            jax.ShapeDtypeStruct((owners * block, width), BF16),
            jax.ShapeDtypeStruct((rows,), jnp.int32),
        ),
        in_specs=[smem(), vmem()],
        out_specs=(vmem(), smem()),
        scratch_shapes=[pltpu.SMEM((2 * owners,), jnp.int32)],
        compiler_params=params(),
        cost_estimate=pl.CostEstimate(flops=0, bytes_accessed=3 * MIB, transcendentals=0),
        name="pack",
    )(codes, flat)
    arrived = lax.all_to_all(sent.reshape(owners, block, width), "roll", split_axis=0, concat_axis=0, tiled=True)

    batch = 8
    part = batch * per_row
    tail_out, tail_lse = pl.pallas_call(
        functools.partial(tail_kernel, steps, per_row, batch, scale),
        out_shape=(
            jax.ShapeDtypeStruct((rows * per_row, width), F32),
            jax.ShapeDtypeStruct((rows, 128), F32),
        ),
        grid=(rows // batch,),
        in_specs=[
            smem(),
            pl.BlockSpec((part, width), lambda i: (i, 0)),
            pl.BlockSpec((batch * slots, width), lambda i: (i, 0)),
            pl.BlockSpec((batch * slots, width), lambda i: (i, 0)),
            pl.BlockSpec((batch * steps, width), lambda i: (i, 0)),
            pl.BlockSpec((batch * steps, width), lambda i: (i, 0)),
        ],
        out_specs=(
            pl.BlockSpec((part, width), lambda i: (i, 0)),
            pl.BlockSpec((batch, 128), lambda i: (i, 0)),
        ),
        compiler_params=params(),
        cost_estimate=pl.CostEstimate(
            flops=4 * rows * per_row * slots * width, bytes_accessed=12 * MIB, transcendentals=rows * per_row * slots
        ),
        name="tail",
    )(
        codes, flat, tail_keys.reshape(rows * slots, width), tail_values.reshape(rows * slots, width),
        new_keys.reshape(rows * steps, width), new_values.reshape(rows * steps, width),
    )

    answered = pl.pallas_call(
        functools.partial(prefix_kernel, cap, per_row, pref, scale),
        out_shape=jax.ShapeDtypeStruct((owners * block, width), BF16),
        in_specs=[vmem(), vmem(), vmem()],
        out_specs=vmem(),
        scratch_shapes=[
            pltpu.VMEM((groups * pref, 2 * width), BF16),
            pltpu.VMEM((owners, 128), jnp.int32),
            pltpu.VMEM((owners * cap, 128), F32),
            pltpu.SMEM((owners, 128), jnp.int32),
            pltpu.SMEM((2, owners * cap + 2 * cap), jnp.int32),
            pltpu.SemaphoreType.DMA,
        ],
        compiler_params=params(),
        cost_estimate=pl.CostEstimate(
            flops=4 * owners * cap * per_row * pref * width, bytes_accessed=6 * MIB,
            transcendentals=owners * cap * per_row * pref,
        ),
        name="prefix",
    )(
        arrived.reshape(owners * block, width), prefix_keys.reshape(groups * pref, width),
        prefix_values.reshape(groups * pref, width),
    )
    back = lax.all_to_all(answered.reshape(owners, block, width), "roll", split_axis=0, concat_axis=0, tiled=True)

    batch = 32
    part = batch * per_row
    merged = pl.pallas_call(
        functools.partial(merge_kernel, cap, per_row, batch),
        out_shape=jax.ShapeDtypeStruct((rows * per_row, width), BF16),
        grid=(rows // batch,),
        in_specs=[
            smem(),
            pl.BlockSpec((owners * block, width), lambda i: (0, 0)),
            pl.BlockSpec((part, width), lambda i: (i, 0)),
            pl.BlockSpec((batch, 128), lambda i: (i, 0)),
        ],
        out_specs=pl.BlockSpec((part, width), lambda i: (i, 0)),
        scratch_shapes=[pltpu.VMEM((owners * cap, 128), F32)],
        compiler_params=params(),
        cost_estimate=pl.CostEstimate(flops=0, bytes_accessed=6 * MIB, transcendentals=0),
        name="merge",
    )(place, back.reshape(owners * block, width), tail_out, tail_lse)
    return merged.reshape(rows, steps, heads, width)


def solution(mesh):
    return jax.shard_map(
        body,
        mesh=mesh,
        in_specs=(
            P("roll", None, "tp", None),
            P("roll", None, "tp", None),
            P("roll", None, "tp", None),
            P("roll", "tp", None, None),
            P("roll", "tp", None, None),
            P("roll", "tp", None, None),
            P("roll", "tp", None, None),
            P("roll", "tp"),
            P("roll", "tp"),
            P("roll", "tp"),
        ),
        out_specs=P("roll", None, "tp", None),
        check_vma=False,
    )
```

time: 215 us -> 134 us (0.62)
  matrix products: 74.2 us -> 0 us
  other arithmetic: 47.9 us -> 0.69 us
  blocking collectives: 14.6 us -> 57.7 us
  Pallas kernels: 0 us -> 33.6 us
  local copies, waits for them, and re-layouts: 23.4 us -> 11.3 us
  starting transfers between devices: 28.7 us -> 16.8 us
  waiting for transfers between devices: 24 us -> 13.3 us
    dot_general x11 -> x0, matrix products: 74.2 us -> none  [the longest x8 67.5 us: product(): jnp.einsum(form, left.astype(jnp.float32), right.astype(jnp.float32), pre...]
    reduce_sum x6 -> x0, other arithmetic: 44.5 us -> none  [the longest x2 38.3 us: prefix_attention(): total = jnp.sum(expo, axis=-1, keepdims=True)]
    all_to_all x0 -> x1, blocking collectives: none -> 41.6 us  [body(): lax.all_to_all(sent.reshape(owners, block, width), 'roll', split_axis=0,...]
    pallas_call x0 -> x4, Pallas kernels: none -> 33.6 us  [the longest x1 16.6 us: body(): pl.pallas_call(functools.partial(prefix_kernel, cap, per_row, pref, scale...]
    all_gather x0 -> x1, blocking collectives: none -> 16.1 us  [body(): codes = lax.all_gather(code, 'tp', axis=0, tiled=True)]
    unnamed x1 -> x0, blocking collectives: 14.6 us -> none
    all_to_all x4 -> x1, starting transfers between devices: 28.7 us -> 16.8 us  [body(): lax.all_to_all(answered.reshape(owners, block, width), 'roll', split_axis...]
    all_to_all x4 -> x1, waiting for transfers between devices: 24 us -> 13.3 us  [body(): lax.all_to_all(answered.reshape(owners, block, width), 'roll', split_axis...]
  transfers between devices with their start and end apart: 4 -> 1, of which waited for: 3 -> 1; matrix products, arithmetic and copies ran while one was open for 27% -> 0% of each run, Pallas kernels for 0% -> 7%
where the time goes in v1:
time: 134 us
  blocking collectives  57.7 us (43%)
  Pallas kernels  33.6 us (25%)
  starting transfers between devices  16.8 us (13%)
  waiting for transfers between devices  13.3 us (10%)
  local copies, waits for them, and re-layouts  11.3 us (8%)
    all_to_all x1, blocking collectives, body(): lax.all_to_all(sent.reshape(owners, block, width), 'roll', split_axis=0,...  41.6 us
    all_to_all x1, starting transfers between devices, body(): lax.all_to_all(answered.reshape(owners, block, width), 'roll', split_axis...  16.8 us
    pallas_call x1, Pallas kernels, body(): pl.pallas_call(functools.partial(prefix_kernel, cap, per_row, pref, scale...  16.6 us
    all_gather x1, blocking collectives, body(): codes = lax.all_gather(code, 'tp', axis=0, tiled=True)  16.1 us
    all_to_all x1, waiting for transfers between devices, body(): lax.all_to_all(answered.reshape(owners, block, width), 'roll', split_axis...  13.3 us
    unnamed x26, local copies, waits for them, and re-layouts  11.3 us
    pallas_call x1, Pallas kernels, body(): pl.pallas_call(functools.partial(tail_kernel, steps, per_row, batch, scal...  9.62 us
    pallas_call x1, Pallas kernels, body(): pl.pallas_call(functools.partial(merge_kernel, cap, per_row, batch), out_...  3.91 us
  transfers between devices with their start and end apart: 1, of which 1 were waited for; matrix products, arithmetic and copies ran while one was open for 0% of the time, Pallas kernels for 7%

profile of v1, /device:TPU:1, one launch (start us, length us, event | category | flops | bytes accessed | tf_op | source)
XLA Modules:
  0.0 133.5 jit_solution(15150710395503651946)
XLA Ops:
  0.0 0.7 add_bitcast_fusion
  0.7 16.1 %all-gather = s32[8,1,16]{2,1,0:T(1,128)S(1)} all-gather(s32[1,1,16]{2,1,0:T(1,128)S(1)} %add_bitcast_fusion), channel_id=1, replica_groups=mesh['roll'=32,'tp'=8] {'tp'}, dimensions={0}, use_global_device_ids=true | all-gather | bytes 576 | tf_op jit(solution)/shard_map/all_gather | solution.py:217
  16.8 0.0 copy-start
  16.8 1.2 copy-done
  18.0 3.5 %pack.1 = (bf16[8704,128]{1,0:T(8,128)(2,1)S(1)}, s32[128]{0:T(128)S(1)}) custom-call(s32[8,16]{1,0:T(8,128)S(1)} %bitcast.25, bf16[4096,128]{1,0:T(8,128)(2,1)S(1)} %bitcast.16), custom_call_target="tpu_custom_call" | custom-call | bytes 3145728 | tf_op jit(solution)/shard_map/pack/pallas_call | solution.py:221
  21.5 0.0 copy-start.11
  21.5 0.0 copy-start.12
  21.5 41.6 %all_to_all.10 = bf16[32,272,128]{2,1,0:T(8,128)(2,1)S(1)} all-to-all(bf16[32,272,128]{2,1,0:T(8,128)(2,1)S(1)} %bitcast.21), channel_id=1, replica_groups=mesh['roll'=32,'tp'=8] {'roll'}, dimensions={0} | all-to-all | bytes 4456448 | tf_op jit(solution)/shard_map/all_to_all | solution.py:234
  63.1 0.0 copy-done.11
  63.1 0.0 copy-done.12
  63.1 16.6 %prefix.1 = bf16[8704,128]{1,0:T(8,128)(2,1)S(1)} custom-call(bf16[8704,128]{1,0:T(8,128)(2,1)S(1)} %bitcast.22, bf16[2048,128]{1,0:T(8,128)(2,1)S(1)} %bitcast.27, bf16[2048,128]{1,0:T(8,128)(2,1)S(1)} %bitcast.28), custom_call_target="tpu_custom_call" | custom-call | flops 4294967296 | bytes 6291456 | tf_op jit(solution)/shard_map/prefix/pallas_call | solution.py:267
  79.7 0.0 copy-start.4
  79.7 1.4 %copy-done.4 = bf16[8704,128]{1,0:T(8,128)(2,1)} copy-done((bf16[8704,128]{1,0:T(8,128)(2,1)}, bf16[8704,128]{1,0:T(8,128)(2,1)S(1)}, u32[]{:S(2)}) %copy-start.4) | copy-done | bytes 2228248
  81.1 0.0 copy-start.1
  81.1 0.0 copy-start.7
  81.1 0.0 copy-start.8
  81.1 16.8 %all-to-all-start.1 = ((bf16[32,272,128]{2,1,0:T(8,128)(2,1)}), bf16[32,272,128]{2,1,0:T(8,128)(2,1)S(1)}, u32[]{:S(2)}, u32[]{:S(2)}) async-start(bf16[32,272,128]{2,1,0:T(8,128)(2,1)} %bitcast.20), calls=%async_computation.1 | async-start | bytes 4456448 | tf_op jit(solution)/shard_map/all_to_all | solution.py:290
  97.9 0.0 copy-done.1
  97.9 0.0 copy-done.7
  97.9 0.0 copy-done.8
  98.0 0.0 copy-start.2
  98.0 2.2 %copy-done.2 = bf16[128,1,128,128]{3,2,1,0:T(8,128)(2,1)S(1)} copy-done((bf16[128,1,128,128]{3,2,1,0:T(8,128)(2,1)S(1)}, bf16[128,1,128,128]{3,2,1,0:T(8,128)(2,1)}, u32[]{:S(2)}) %copy-start.2) | copy-done | bytes 4194328
  100.2 0.0 copy-start.3
  100.2 2.2 %copy-done.3 = bf16[128,1,128,128]{3,2,1,0:T(8,128)(2,1)S(1)} copy-done((bf16[128,1,128,128]{3,2,1,0:T(8,128)(2,1)S(1)}, bf16[128,1,128,128]{3,2,1,0:T(8,128)(2,1)}, u32[]{:S(2)}) %copy-start.3) | copy-done | bytes 4194328
  102.3 9.6 %tail.1 = (f32[4096,128]{1,0:T(8,128)S(1)}, f32[128,128]{1,0:T(8,128)S(1)}) custom-call(s32[8,16]{1,0:T(8,128)S(1)} %bitcast.26, bf16[4096,128]{1,0:T(8,128)(2,1)S(1)} %bitcast.17, bf16[16384,128]{1,0:T(8,128)(2,1)S(1)} %bitcast.18, bf16[16384,128]{1,0:T(8,128)(2,1)S(1)} %bitcast.19, bf16[512,128]{1,0:T(8,128)(2,1)S(1)} %bitcast.23, ...), custom_call_target="tpu_custom_call" | custom-call | flops 268435456 | bytes 12582912 | tf_op jit(solution)/shard_map/tail/pallas_call | solution.py:238
  112.0 0.0 copy-start.5
  112.0 1.3 copy-done.5
  113.3 0.0 copy-start.9
  113.3 0.6 copy-done.9
  113.9 13.3 %all-to-all-done.1 = bf16[32,272,128]{2,1,0:T(8,128)(2,1)S(1)} async-done(((bf16[32,272,128]{2,1,0:T(8,128)(2,1)}), bf16[32,272,128]{2,1,0:T(8,128)(2,1)S(1)}, u32[]{:S(2)}, u32[]{:S(2)}) %all-to-all-start.1) | async-done | bytes 2228256 | tf_op jit(solution)/shard_map/all_to_all | solution.py:290
  127.2 0.0 copy-start.6
  127.2 1.6 %copy-done.6 = f32[4096,128]{1,0:T(8,128)S(1)} copy-done((f32[4096,128]{1,0:T(8,128)S(1)}, f32[4096,128]{1,0:T(8,128)}, u32[]{:S(2)}) %copy-start.6) | copy-done | bytes 2097176
  128.8 0.0 copy-start.10
  128.8 0.8 copy-done.10
  129.6 3.9 %merge.1 = bf16[4096,128]{1,0:T(8,128)(2,1)} custom-call(s32[128]{0:T(128)S(1)} %get-tuple-element.9.place_ref, bf16[8704,128]{1,0:T(8,128)(2,1)S(1)} %bitcast.15, f32[4096,128]{1,0:T(8,128)S(1)} %copy-done.6, f32[128,128]{1,0:T(8,128)S(1)} %copy-done.10), custom_call_target="tpu_custom_call" | custom-call | bytes 6291456 | tf_op jit(solution)/shard_map/merge/pallas_call | solution.py:294
Async XLA Ops:
  16.8 1.2 copy-start
  21.5 41.6 %copy-start.11 = (bf16[2,1,1024,128]{3,2,1,0:T(8,128)(2,1)S(1)}, bf16[2,1,1024,128]{3,2,1,0:T(8,128)(2,1)}, u32[]{:S(2)}) copy-start(bf16[2,1,1024,128]{3,2,1,0:T(8,128)(2,1)} %param.15) | copy-start | bytes 1572868
  21.5 41.6 %copy-start.12 = (bf16[2,1,1024,128]{3,2,1,0:T(8,128)(2,1)S(1)}, bf16[2,1,1024,128]{3,2,1,0:T(8,128)(2,1)}, u32[]{:S(2)}) copy-start(bf16[2,1,1024,128]{3,2,1,0:T(8,128)(2,1)} %param.16) | copy-start | bytes 1572868
  79.7 1.4 %copy-start.4 = (bf16[8704,128]{1,0:T(8,128)(2,1)}, bf16[8704,128]{1,0:T(8,128)(2,1)S(1)}, u32[]{:S(2)}) copy-start(bf16[8704,128]{1,0:T(8,128)(2,1)S(1)} %prefix.1) | copy-start | bytes 6684676
  81.1 16.8 %copy-start.1 = (bf16[128,4,8,128]{3,2,1,0:T(8,128)(2,1)S(1)}, bf16[128,4,8,128]{3,2,1,0:T(8,128)(2,1)}, u32[]{:S(2)}) copy-start(bf16[128,4,8,128]{3,2,1,0:T(8,128)(2,1)} %param.10) | copy-start | bytes 3145732
  81.1 16.8 %copy-start.7 = (bf16[128,4,1,128]{3,1,2,0:T(4,128)(2,1)S(1)}, bf16[128,4,1,128]{3,1,2,0:T(4,128)(2,1)}, u32[]{:S(2)}) copy-start(bf16[128,4,1,128]{3,1,2,0:T(4,128)(2,1)} %param.11) | copy-start | bytes 393220
  81.1 16.8 %copy-start.8 = (bf16[128,4,1,128]{3,1,2,0:T(4,128)(2,1)S(1)}, bf16[128,4,1,128]{3,1,2,0:T(4,128)(2,1)}, u32[]{:S(2)}) copy-start(bf16[128,4,1,128]{3,1,2,0:T(4,128)(2,1)} %param.12) | copy-start | bytes 393220
  81.1 46.1 %all-to-all-start.1 = ((bf16[32,272,128]{2,1,0:T(8,128)(2,1)}), bf16[32,272,128]{2,1,0:T(8,128)(2,1)S(1)}, u32[]{:S(2)}, u32[]{:S(2)}) async-start(bf16[32,272,128]{2,1,0:T(8,128)(2,1)} %bitcast.20), calls=%async_computation.1 | async-start | bytes 4456448 | tf_op jit(solution)/shard_map/all_to_all | solution.py:290
  98.0 2.2 %copy-start.2 = (bf16[128,1,128,128]{3,2,1,0:T(8,128)(2,1)S(1)}, bf16[128,1,128,128]{3,2,1,0:T(8,128)(2,1)}, u32[]{:S(2)}) copy-start(bf16[128,1,128,128]{3,2,1,0:T(8,128)(2,1)} %param.13) | copy-start | bytes 12582916
  100.2 2.2 %copy-start.3 = (bf16[128,1,128,128]{3,2,1,0:T(8,128)(2,1)S(1)}, bf16[128,1,128,128]{3,2,1,0:T(8,128)(2,1)}, u32[]{:S(2)}) copy-start(bf16[128,1,128,128]{3,2,1,0:T(8,128)(2,1)} %param.14) | copy-start | bytes 12582916
  112.0 1.3 copy-start.5
  113.3 0.6 copy-start.9
  127.2 1.6 %copy-start.6 = (f32[4096,128]{1,0:T(8,128)S(1)}, f32[4096,128]{1,0:T(8,128)}, u32[]{:S(2)}) copy-start(f32[4096,128]{1,0:T(8,128)} %copy-done.5) | copy-start | bytes 6291460
  128.8 0.8 copy-start.10

commit v2 on v1

v2 whole, which is shorter than its diff:
```python
import functools
import math

import jax
import jax.numpy as jnp
from jax import lax
from jax.experimental import pallas as pl
from jax.experimental.pallas import tpu as pltpu
from jax.sharding import PartitionSpec as P

LOG2E = math.log2(math.e)
MIB = 1 << 20
F32 = jnp.float32
BF16 = jnp.bfloat16
EXTRA = 16


def lane_group_mask(per_row, width):
    sub = lax.broadcasted_iota(jnp.int32, (per_row, width), 0)
    lane = lax.broadcasted_iota(jnp.int32, (per_row, width), 1)
    return (lane % per_row) == sub


def pack_kernel(cap, per_row, code_ref, q_ref, out_ref, place_ref, held_ref, extra_ref, where_ref, sems):
    lines, line = code_ref.shape
    rows = lines * line
    owners = out_ref.shape[0]
    load = pltpu.make_async_copy(q_ref, held_ref, sems.at[0])
    load.start()
    group = lax.shift_right_logical(code_ref[...], 8).astype(F32).astype(BF16)
    z = lax.broadcasted_iota(jnp.int32, (lines, rows), 0)
    r = lax.broadcasted_iota(jnp.int32, (lines, rows), 1)
    j = lax.broadcasted_iota(jnp.int32, (line, rows), 0)
    rj = lax.broadcasted_iota(jnp.int32, (line, rows), 1)
    spread = jnp.dot(group, (rj % line == j).astype(BF16), preferred_element_type=F32)
    across = jnp.sum(jnp.where(r // line == z, spread, 0.0), axis=0, keepdims=True)
    rz = lax.broadcasted_iota(jnp.int32, (rows, lines), 0)
    zz = lax.broadcasted_iota(jnp.int32, (rows, lines), 1)
    picked = jnp.dot((rz // line == zz).astype(BF16), group, preferred_element_type=F32)
    rl = lax.broadcasted_iota(jnp.int32, (rows, line), 0)
    jl = lax.broadcasted_iota(jnp.int32, (rows, line), 1)
    picked = jnp.where(rl % line == jl, picked, 0.0).astype(BF16)
    down = jnp.dot(picked, jnp.ones((line, rows), BF16), preferred_element_type=F32)
    earlier = lax.broadcasted_iota(jnp.int32, (rows, rows), 0) < lax.broadcasted_iota(jnp.int32, (rows, rows), 1)
    rank = jnp.sum(jnp.where((down == across) & earlier, 1.0, 0.0), axis=0, keepdims=True).astype(jnp.int32)
    whole = across.astype(jnp.int32)
    slot = jnp.where((whole & 1) == 1, cap - 1 - rank, rank)
    place = lax.shift_right_logical(whole, 1) * cap + slot
    place_ref[...] = place
    index = pltpu.make_async_copy(place_ref, where_ref, sems.at[1])
    index.start()
    named = lax.broadcasted_iota(jnp.int32, (2 * owners, rows), 0).astype(F32) == across
    counts = jnp.dot(named.astype(BF16), jnp.ones((rows, 128), BF16), preferred_element_type=F32)
    half = EXTRA // 2
    for o in range(owners):
        first = jnp.broadcast_to(counts[2 * o:2 * o + 1, :], (half, 128))
        second = jnp.broadcast_to(counts[2 * o + 1:2 * o + 2, :], (half, 128))
        extra_ref[o] = jnp.concatenate([first, second], axis=0).astype(BF16)
    more = pltpu.make_async_copy(extra_ref, out_ref.at[:, pl.ds(cap * per_row, EXTRA), :], sems.at[2])
    more.start()
    index.wait()
    load.wait()

    def one(i, carry):
        at = where_ref[0, i]
        pltpu.make_async_copy(
            held_ref.at[pl.ds(pl.multiple_of(i * per_row, per_row), per_row), :],
            out_ref.at[lax.shift_right_logical(at, 3), pl.ds(pl.multiple_of((at & 7) * per_row, per_row), per_row), :],
            sems.at[0],
        ).start()
        return carry

    lax.fori_loop(0, rows, one, 0, unroll=8)
    more.wait()
    load.wait()


def tail_kernel(steps, per_row, batch, scale, code_ref, q_ref, tk_ref, tv_ref, nk_ref, nv_ref, out_ref, lse_ref):
    base = pl.program_id(0) * batch
    line = code_ref.shape[1]
    slots = tk_ref.shape[0] // batch
    heads = per_row // steps
    total_rows = batch * per_row
    q = q_ref[...]
    parts = []
    lane = lax.broadcasted_iota(jnp.int32, (per_row, slots), 1)
    for i in range(batch):
        r = base + i
        length = code_ref[r // line, r % line] & 255
        s = lax.dot_general(
            q[i * per_row:(i + 1) * per_row], tk_ref[i * slots:(i + 1) * slots, :],
            (((1,), (1,)), ((), ())), preferred_element_type=F32,
        )
        parts.append(jnp.where(lane < length, s, -jnp.inf))
    st = jnp.concatenate(parts, axis=0)
    sn = lax.dot_general(q, nk_ref[...], (((1,), (1,)), ((), ())), preferred_element_type=F32)
    row = lax.broadcasted_iota(jnp.int32, sn.shape, 0)
    col = lax.broadcasted_iota(jnp.int32, sn.shape, 1)
    own = (row // per_row) == (col // steps)
    causal = (col % steps) <= ((row % per_row) // heads)
    sn = jnp.where(own & causal, sn, -jnp.inf)
    top = jnp.maximum(jnp.max(st, axis=1, keepdims=True), jnp.max(sn, axis=1, keepdims=True))
    et = jnp.exp2((st - top) * (scale * LOG2E))
    en = jnp.exp2((sn - top) * (scale * LOG2E))
    total = jnp.sum(et, axis=1, keepdims=True) + jnp.sum(en, axis=1, keepdims=True)
    pt = et.astype(BF16)
    summed = jnp.concatenate(
        [
            jnp.dot(pt[i * per_row:(i + 1) * per_row], tv_ref[i * slots:(i + 1) * slots, :], preferred_element_type=F32)
            for i in range(batch)
        ],
        axis=0,
    )
    summed = summed + jnp.dot(en.astype(BF16), nv_ref[...], preferred_element_type=F32)
    out_ref[...] = summed / total
    lse = top * scale + jnp.log(total)
    mask = lane_group_mask(per_row, 128)
    for i in range(batch):
        one = jnp.where(mask, lse[i * per_row:(i + 1) * per_row], 0.0)
        lse_ref[i:i + 1, :] = jnp.sum(one, axis=0, keepdims=True)


def prefix_kernel(
    cap, per_row, pref, scale, x_ref, k_ref, v_ref, out_ref, held_ref, wide_ref, list_ref, lse_ref, sent_ref, where_ref, sems
):
    sources = x_ref.shape[0]
    data = cap * per_row
    groups = v_ref.shape[0] // pref
    half = EXTRA // 2
    i = lax.broadcasted_iota(jnp.int32, (sources, sources), 0)
    j = lax.broadcasted_iota(jnp.int32, (sources, sources), 1)
    lower = (j <= i).astype(BF16)
    lane = lax.broadcasted_iota(jnp.int32, (1, 128), 1)
    entries = []
    totals = []
    for g in range(2):
        count = jnp.concatenate(
            [x_ref[s, data:data + EXTRA, :].astype(F32)[g * half:g * half + 1, :] for s in range(sources)], axis=0
        )
        ends = jnp.dot(lower, count.astype(BF16), preferred_element_type=F32)
        total = ends[sources - 1:sources, :]
        totals.append(total)
        for h in range(2):
            at = jnp.maximum(jnp.minimum((lane + 128 * h).astype(F32), total - 1.0), 0.0)
            passed = ends <= at
            source = jnp.sum(jnp.where(passed, 1.0, 0.0), axis=0, keepdims=True)
            within = at - jnp.sum(jnp.where(passed, count, 0.0), axis=0, keepdims=True)
            entries.append(source * cap + (within if g == 0 else (cap - 1) - within))
    list_ref[...] = jnp.concatenate(entries + totals + totals, axis=0).astype(jnp.int32)
    copy = pltpu.make_async_copy(list_ref, where_ref, sems.at[0])
    copy.start()
    wide_ref[:, 0:128] = v_ref[...]
    wide_ref[:, 128:256] = jnp.ones((groups * pref, 128), BF16)
    lse_ref[...] = jnp.zeros(lse_ref.shape, F32)
    copy.wait()
    found = [where_ref[4, 0], where_ref[5, 0]]
    mask = lane_group_mask(per_row, 128)
    factor = scale * LOG2E

    def attend(unit, sub, shifted):
        first_units = (found[0] + unit - 1) // unit
        units = first_units + (found[1] + unit - 1) // unit

        def one(b, carry):
            g = (b >= first_units).astype(jnp.int32)
            j = (b - g * first_units) * unit
            row = 2 * g + lax.shift_right_logical(j, 7)
            first = j & 127
            slots = [where_ref[row, first + i] for i in range(unit)]
            own = [lax.shift_right_logical(s, 3) for s in slots]
            start = [pl.multiple_of((s & 7) * per_row, per_row) for s in slots]
            here = pl.multiple_of(g * pref, pref)
            scores = []
            for t in range(0, unit, sub):
                q = jnp.concatenate([x_ref[own[i], pl.ds(start[i], per_row), :] for i in range(t, t + sub)], axis=0)
                scores.append(
                    lax.dot_general(
                        q, k_ref[pl.ds(here, pref), :], (((1,), (1,)), ((), ())), preferred_element_type=F32
                    )
                )
            low, high = carry
            for t in range(0, unit, sub):
                score = scores[t // sub]
                top = jnp.max(score, axis=1, keepdims=True) if shifted else None
                expo = jnp.exp2((score - top if shifted else score) * factor).astype(BF16)
                both = jnp.dot(expo, wide_ref[pl.ds(here, pref), :], preferred_element_type=F32)
                total = both[:, 128:256]
                result = (both[:, 0:128] / total).astype(BF16)
                lse = jnp.log(total)
                if shifted:
                    lse = lse + top * scale
                stacked = total.reshape(sub * per_row // 8, 8, 128)
                low = jnp.minimum(low, jnp.min(stacked, axis=0))
                high = jnp.maximum(high, jnp.max(stacked, axis=0))
                for i in range(sub):
                    part = slice(i * per_row, (i + 1) * per_row)
                    held_ref[own[t + i], pl.ds(start[t + i], per_row), :] = result[part]
                    lse_ref[pl.ds(slots[t + i], 1), :] = jnp.sum(
                        jnp.where(mask, lse[part], 0.0), axis=0, keepdims=True
                    )
            return low, high

        return lax.fori_loop(0, units, one, (jnp.ones((8, 128), F32), jnp.ones((8, 128), F32)))

    low, high = attend(32, 8, False)
    safe = (jnp.min(low) > 2.0**-70) & (jnp.max(high) < 2.0**100)

    @pl.when(jnp.logical_not(safe))
    def _():
        attend(8, 8, True)

    for s in range(sources):
        full = lse_ref[s * cap:(s + 1) * cap, :]
        high_part = full.astype(BF16).astype(F32)
        rest = full - high_part
        mid_part = rest.astype(BF16).astype(F32)
        low_part = rest - mid_part
        lanes = lax.broadcasted_iota(jnp.int32, full.shape, 1)
        sent = jnp.where(lanes < per_row, high_part, jnp.where(lanes < 2 * per_row, mid_part, low_part))
        held_ref[s, data:data + EXTRA, :] = jnp.concatenate([sent, jnp.zeros_like(sent)], axis=0).astype(BF16)
    out = pltpu.make_async_copy(held_ref, out_ref, sems.at[0])
    out.start()
    out.wait()


def merge_kernel(cap, per_row, batch, place_ref, x_ref, tail_ref, lse_ref, out_ref, sent_ref, weight_ref):
    owners = x_ref.shape[0]
    data = cap * per_row
    step = pl.program_id(0)

    @pl.when(step == 0)
    def _():
        for o in range(owners):
            sent_ref[o * cap:(o + 1) * cap, :] = x_ref[o, data:data + EXTRA, :].astype(F32)[0:cap, :]

    mask = lane_group_mask(per_row, 128)
    lane = lax.broadcasted_iota(jnp.int32, (batch, 128), 1)
    places = [place_ref[0, step * batch + i] for i in range(batch)]
    lse = jnp.concatenate([sent_ref[pl.ds(p, 1), :] for p in places], axis=0)
    terms = jnp.where(lane < 3 * per_row, lse, -lse_ref[...])
    ahead = terms
    for k in range(1, 4):
        ahead = ahead + pltpu.roll(terms, k * per_row, 1)
    weight = 1.0 / (1.0 + jnp.exp(-ahead))
    high = weight.astype(BF16).astype(F32)
    mid = (weight - high).astype(BF16).astype(F32)
    weight_ref[...] = jnp.where(lane < per_row, high, jnp.where(lane < 2 * per_row, mid, jnp.where(lane < 3 * per_row, weight - high - mid, 0.0)))
    ones = jnp.ones((128, 128), BF16)
    for i in range(batch):
        place = places[i]
        spread = jnp.where(mask, weight_ref[i:i + 1, :], 0.0).astype(BF16)
        weight_p = jnp.dot(spread, ones, preferred_element_type=F32)
        start = pl.multiple_of((place & 7) * per_row, per_row)
        prefix = x_ref[lax.shift_right_logical(place, 3), pl.ds(start, per_row), :].astype(F32)
        tail = tail_ref[i * per_row:(i + 1) * per_row, :]
        out_ref[i * per_row:(i + 1) * per_row, :] = (tail + weight_p * (prefix - tail)).astype(BF16)


def vmem():
    return pl.BlockSpec(memory_space=pltpu.VMEM)


def hbm():
    return pl.BlockSpec(memory_space=pltpu.MemorySpace.HBM)


def smem():
    return pl.BlockSpec(memory_space=pltpu.SMEM)


def body(
    queries, new_keys, new_values, tail_keys, tail_values, prefix_keys, prefix_values, route_owner, group_slot, tail_len
):
    rows, steps, heads, width = queries.shape
    owners = lax.axis_size("roll")
    cap = 8
    per_row = steps * heads
    scale = 1.0 / math.sqrt(width)
    slots = tail_keys.shape[2]
    pref = prefix_keys.shape[2]
    groups = prefix_keys.shape[0]
    block = cap * per_row + EXTRA
    code = (route_owner * 2 + group_slot) * 256 + tail_len
    codes = lax.all_gather(code, "tp", axis=0, tiled=True)
    flat = queries.reshape(rows * per_row, width)
    params = functools.partial(pltpu.CompilerParams, vmem_limit_bytes=32 * MIB)

    sent, place = pl.pallas_call(
        functools.partial(pack_kernel, cap, per_row),
        out_shape=(
            jax.ShapeDtypeStruct((owners, block, width), BF16),
            jax.ShapeDtypeStruct((1, rows), jnp.int32),
        ),
        in_specs=[vmem(), hbm()],
        out_specs=(hbm(), vmem()),
        scratch_shapes=[
            pltpu.VMEM((rows * per_row, width), BF16),
            pltpu.VMEM((owners, EXTRA, 128), BF16),
            pltpu.SMEM((1, rows), jnp.int32),
            pltpu.SemaphoreType.DMA((3,)),
        ],
        compiler_params=params(),
        cost_estimate=pl.CostEstimate(flops=0, bytes_accessed=3 * MIB, transcendentals=0),
        name="pack",
    )(codes, flat)
    arrived = lax.all_to_all(sent, "roll", split_axis=0, concat_axis=0, tiled=True)

    batch = 8
    part = batch * per_row
    tail_out, tail_lse = pl.pallas_call(
        functools.partial(tail_kernel, steps, per_row, batch, scale),
        out_shape=(
            jax.ShapeDtypeStruct((rows * per_row, width), F32),
            jax.ShapeDtypeStruct((rows, 128), F32),
        ),
        grid=(rows // batch,),
        in_specs=[
            smem(),
            pl.BlockSpec((part, width), lambda i: (i, 0)),
            pl.BlockSpec((batch * slots, width), lambda i: (i, 0)),
            pl.BlockSpec((batch * slots, width), lambda i: (i, 0)),
            pl.BlockSpec((batch * steps, width), lambda i: (i, 0)),
            pl.BlockSpec((batch * steps, width), lambda i: (i, 0)),
        ],
        out_specs=(
            pl.BlockSpec((part, width), lambda i: (i, 0)),
            pl.BlockSpec((batch, 128), lambda i: (i, 0)),
        ),
        compiler_params=params(),
        cost_estimate=pl.CostEstimate(
            flops=4 * rows * per_row * slots * width, bytes_accessed=12 * MIB, transcendentals=rows * per_row * slots
        ),
        name="tail",
    )(
        codes, flat, tail_keys.reshape(rows * slots, width), tail_values.reshape(rows * slots, width),
        new_keys.reshape(rows * steps, width), new_values.reshape(rows * steps, width),
    )

    answered = pl.pallas_call(
        functools.partial(prefix_kernel, cap, per_row, pref, scale),
        out_shape=jax.ShapeDtypeStruct((owners, block, width), BF16),
        in_specs=[vmem(), vmem(), vmem()],
        out_specs=hbm(),
        scratch_shapes=[
            pltpu.VMEM((owners, block, width), BF16),
            pltpu.VMEM((groups * pref, 2 * width), BF16),
            pltpu.VMEM((8, 128), jnp.int32),
            pltpu.VMEM((owners * cap, 128), F32),
            pltpu.VMEM((owners * cap, 128), F32),
            pltpu.SMEM((8, 128), jnp.int32),
            pltpu.SemaphoreType.DMA((1,)),
        ],
        compiler_params=params(),
        cost_estimate=pl.CostEstimate(
            flops=4 * owners * cap * per_row * pref * width, bytes_accessed=6 * MIB,
            transcendentals=owners * cap * per_row * pref,
        ),
        name="prefix",
    )(arrived, prefix_keys.reshape(groups * pref, width), prefix_values.reshape(groups * pref, width))
    back = lax.all_to_all(answered, "roll", split_axis=0, concat_axis=0, tiled=True)

    batch = 32
    part = batch * per_row
    merged = pl.pallas_call(
        functools.partial(merge_kernel, cap, per_row, batch),
        out_shape=jax.ShapeDtypeStruct((rows * per_row, width), BF16),
        grid=(rows // batch,),
        in_specs=[
            smem(),
            pl.BlockSpec((owners, block, width), lambda i: (0, 0, 0)),
            pl.BlockSpec((part, width), lambda i: (i, 0)),
            pl.BlockSpec((batch, 128), lambda i: (i, 0)),
        ],
        out_specs=pl.BlockSpec((part, width), lambda i: (i, 0)),
        scratch_shapes=[pltpu.VMEM((owners * cap, 128), F32), pltpu.VMEM((batch, 128), F32)],
        compiler_params=params(),
        cost_estimate=pl.CostEstimate(flops=0, bytes_accessed=6 * MIB, transcendentals=0),
        name="merge",
    )(place, back, tail_out, tail_lse)
    return merged.reshape(rows, steps, heads, width)


def solution(mesh):
    return jax.shard_map(
        body,
        mesh=mesh,
        in_specs=(
            P("roll", None, "tp", None),
            P("roll", None, "tp", None),
            P("roll", None, "tp", None),
            P("roll", "tp", None, None),
            P("roll", "tp", None, None),
            P("roll", "tp", None, None),
            P("roll", "tp", None, None),
            P("roll", "tp"),
            P("roll", "tp"),
            P("roll", "tp"),
        ),
        out_specs=P("roll", None, "tp", None),
        check_vma=False,
    )
```

time: 134 us -> 144 us (1.075)
  starting transfers between devices: 16.8 us -> 25.1 us
  Pallas kernels: 33.6 us -> 36.4 us
    all_to_all x1, starting transfers between devices: 16.8 us -> 25.1 us  [body(): lax.all_to_all(answered, 'roll', split_axis=0, concat_axis=0, tiled=True)]
    pallas_call x1, Pallas kernels: 16.6 us -> 20.2 us  [body(): pl.pallas_call(functools.partial(prefix_kernel, cap, per_row, pref, scale...]
where the time goes in v2:
time: 144 us; the launch traced here: 145 us
  blocking collectives  57.7 us (40%)
  Pallas kernels  36.4 us (25%)
  starting transfers between devices  25.1 us (17%)
  waiting for transfers between devices  13.4 us (9%)
  local copies, waits for them, and re-layouts  11.3 us (8%)
    all_to_all x1, blocking collectives, body(): lax.all_to_all(sent, 'roll', split_axis=0, concat_axis=0, tiled=True)  41.6 us
    all_to_all x1, starting transfers between devices, body(): lax.all_to_all(answered, 'roll', split_axis=0, concat_axis=0, tiled=True)  25.1 us
    pallas_call x1, Pallas kernels, body(): pl.pallas_call(functools.partial(prefix_kernel, cap, per_row, pref, scale...  20.2 us
    all_gather x1, blocking collectives, body(): codes = lax.all_gather(code, 'tp', axis=0, tiled=True)  16.1 us
    all_to_all x1, waiting for transfers between devices, body(): lax.all_to_all(answered, 'roll', split_axis=0, concat_axis=0, tiled=True)  13.4 us
    unnamed x26, local copies, waits for them, and re-layouts  11.3 us
    pallas_call x1, Pallas kernels, body(): pl.pallas_call(functools.partial(tail_kernel, steps, per_row, batch, scal...  9.63 us
    pallas_call x1, Pallas kernels, body(): pl.pallas_call(functools.partial(merge_kernel, cap, per_row, batch), out_...  3.48 us
  transfers between devices with their start and end apart: 1, of which 1 were waited for; matrix products, arithmetic and copies ran while one was open for 0% of the time, Pallas kernels for 7%

profile of v2, /device:TPU:1, one launch (start us, length us, event | category | flops | bytes accessed | tf_op | source)
XLA Modules:
  0.0 144.7 jit_solution(11466122733989611400)
XLA Ops:
  0.0 0.7 add_bitcast_fusion
  0.7 16.1 %all-gather = s32[8,1,16]{2,1,0:T(1,128)S(1)} all-gather(s32[1,1,16]{2,1,0:T(1,128)S(1)} %add_bitcast_fusion), channel_id=1, replica_groups=mesh['roll'=32,'tp'=8] {'tp'}, dimensions={0}, use_global_device_ids=true | all-gather | bytes 576 | tf_op jit(solution)/shard_map/all_gather | solution.py:284
  16.8 0.0 copy-start
  16.8 1.2 copy-done
  18.0 3.1 %pack.1 = (bf16[32,272,128]{2,1,0:T(8,128)(2,1)S(1)}, s32[1,128]{1,0:T(1,128)S(1)}) custom-call(s32[8,16]{1,0:T(8,128)S(1)} %bitcast.17, bf16[4096,128]{1,0:T(8,128)(2,1)S(1)} %bitcast.11), custom_call_target="tpu_custom_call" | custom-call | bytes 3145728 | tf_op jit(solution)/shard_map/pack/pallas_call | solution.py:288
  21.1 0.0 copy-start.11
  21.1 0.0 copy-start.12
  21.1 41.6 %all_to_all.10.x_ref = bf16[32,272,128]{2,1,0:T(8,128)(2,1)S(1)} all-to-all(bf16[32,272,128]{2,1,0:T(8,128)(2,1)S(1)} %get-tuple-element.10), channel_id=1, replica_groups=mesh['roll'=32,'tp'=8] {'roll'}, dimensions={0} | all-to-all | bytes 4456448 | tf_op jit(solution)/shard_map/all_to_all | solution.py:306
  62.7 0.0 copy-done.11
  62.7 0.0 copy-done.12
  62.7 20.2 %prefix.1 = bf16[32,272,128]{2,1,0:T(8,128)(2,1)S(1)} custom-call(bf16[32,272,128]{2,1,0:T(8,128)(2,1)S(1)} %all_to_all.10.x_ref, bf16[2048,128]{1,0:T(8,128)(2,1)S(1)} %bitcast.19, bf16[2048,128]{1,0:T(8,128)(2,1)S(1)} %bitcast.20), custom_call_target="tpu_custom_call" | custom-call | flops 4294967296 | bytes 6291456 | tf_op jit(solution)/shard_map/prefix/pallas_call | solution.py:339
  82.9 0.0 copy-start.4
  82.9 1.4 copy-done.4
  84.3 0.0 copy-start.1
  84.3 0.0 copy-start.7
  84.3 0.0 copy-start.8
  84.3 25.1 %all-to-all-start.1 = ((bf16[32,272,128]{2,1,0:T(8,128)(2,1)}), bf16[32,272,128]{2,1,0:T(8,128)(2,1)S(1)}, u32[]{:S(2)}, u32[]{:S(2)}) async-start(bf16[32,272,128]{2,1,0:T(8,128)(2,1)} %copy-done.4), calls=%async_computation.1 | async-start | bytes 4456448 | tf_op jit(solution)/shard_map/all_to_all | solution.py:360
  109.4 0.0 copy-done.1
  109.4 0.0 copy-done.7
  109.4 0.0 copy-done.8
  109.4 0.0 copy-start.2
  109.5 2.2 %copy-done.2 = bf16[128,1,128,128]{3,2,1,0:T(8,128)(2,1)S(1)} copy-done((bf16[128,1,128,128]{3,2,1,0:T(8,128)(2,1)S(1)}, bf16[128,1,128,128]{3,2,1,0:T(8,128)(2,1)}, u32[]{:S(2)}) %copy-start.2) | copy-done | bytes 4194328
  111.6 0.0 copy-start.3
  111.6 2.2 %copy-done.3 = bf16[128,1,128,128]{3,2,1,0:T(8,128)(2,1)S(1)} copy-done((bf16[128,1,128,128]{3,2,1,0:T(8,128)(2,1)S(1)}, bf16[128,1,128,128]{3,2,1,0:T(8,128)(2,1)}, u32[]{:S(2)}) %copy-start.3) | copy-done | bytes 4194328
  113.8 9.6 %tail.1 = (f32[4096,128]{1,0:T(8,128)S(1)}, f32[128,128]{1,0:T(8,128)S(1)}) custom-call(s32[8,16]{1,0:T(8,128)S(1)} %bitcast.18, bf16[4096,128]{1,0:T(8,128)(2,1)S(1)} %bitcast.12, bf16[16384,128]{1,0:T(8,128)(2,1)S(1)} %bitcast.13, bf16[16384,128]{1,0:T(8,128)(2,1)S(1)} %bitcast.14, bf16[512,128]{1,0:T(8,128)(2,1)S(1)} %bitcast.15, ...), custom_call_target="tpu_custom_call" | custom-call | flops 268435456 | bytes 12582912 | tf_op jit(solution)/shard_map/tail/pallas_call | solution.py:310
  123.5 0.0 copy-start.5
  123.5 1.3 copy-done.5
  124.8 0.0 copy-start.9
  124.8 0.6 copy-done.9
  125.4 13.4 %all-to-all-done.1.x_ref = bf16[32,272,128]{2,1,0:T(8,128)(2,1)S(1)} async-done(((bf16[32,272,128]{2,1,0:T(8,128)(2,1)}), bf16[32,272,128]{2,1,0:T(8,128)(2,1)S(1)}, u32[]{:S(2)}, u32[]{:S(2)}) %all-to-all-start.1) | async-done | bytes 2228256 | tf_op jit(solution)/shard_map/all_to_all | solution.py:360
  138.8 0.0 copy-start.6
  138.8 1.6 %copy-done.6 = f32[4096,128]{1,0:T(8,128)S(1)} copy-done((f32[4096,128]{1,0:T(8,128)S(1)}, f32[4096,128]{1,0:T(8,128)}, u32[]{:S(2)}) %copy-start.6) | copy-done | bytes 2097176
  140.4 0.0 copy-start.10
  140.4 0.8 copy-done.10
  141.2 3.5 %merge.1 = bf16[4096,128]{1,0:T(8,128)(2,1)} custom-call(s32[1,128]{1,0:T(1,128)S(1)} %get-tuple-element.9.place_ref, bf16[32,272,128]{2,1,0:T(8,128)(2,1)S(1)} %all-to-all-done.1.x_ref, f32[4096,128]{1,0:T(8,128)S(1)} %copy-done.6, f32[128,128]{1,0:T(8,128)S(1)} %copy-done.10), custom_call_target="tpu_custom_call" | custom-call | bytes 6291456 | tf_op jit(solution)/shard_map/merge/pallas_call | solution.py:364
Async XLA Ops:
  16.8 1.2 copy-start
  21.1 41.6 %copy-start.11 = (bf16[2,1,1024,128]{3,2,1,0:T(8,128)(2,1)S(1)}, bf16[2,1,1024,128]{3,2,1,0:T(8,128)(2,1)}, u32[]{:S(2)}) copy-start(bf16[2,1,1024,128]{3,2,1,0:T(8,128)(2,1)} %param.15) | copy-start | bytes 1572868
  21.1 41.6 %copy-start.12 = (bf16[2,1,1024,128]{3,2,1,0:T(8,128)(2,1)S(1)}, bf16[2,1,1024,128]{3,2,1,0:T(8,128)(2,1)}, u32[]{:S(2)}) copy-start(bf16[2,1,1024,128]{3,2,1,0:T(8,128)(2,1)} %param.16) | copy-start | bytes 1572868
  82.9 1.4 copy-start.4
  84.3 25.1 %copy-start.1 = (bf16[128,4,8,128]{3,2,1,0:T(8,128)(2,1)S(1)}, bf16[128,4,8,128]{3,2,1,0:T(8,128)(2,1)}, u32[]{:S(2)}) copy-start(bf16[128,4,8,128]{3,2,1,0:T(8,128)(2,1)} %param.10) | copy-start | bytes 3145732
  84.3 25.1 %copy-start.7 = (bf16[128,4,1,128]{3,1,2,0:T(4,128)(2,1)S(1)}, bf16[128,4,1,128]{3,1,2,0:T(4,128)(2,1)}, u32[]{:S(2)}) copy-start(bf16[128,4,1,128]{3,1,2,0:T(4,128)(2,1)} %param.11) | copy-start | bytes 393220
  84.3 25.2 %copy-start.8 = (bf16[128,4,1,128]{3,1,2,0:T(4,128)(2,1)S(1)}, bf16[128,4,1,128]{3,1,2,0:T(4,128)(2,1)}, u32[]{:S(2)}) copy-start(bf16[128,4,1,128]{3,1,2,0:T(4,128)(2,1)} %param.12) | copy-start | bytes 393220
  84.3 54.5 %all-to-all-start.1 = ((bf16[32,272,128]{2,1,0:T(8,128)(2,1)}), bf16[32,272,128]{2,1,0:T(8,128)(2,1)S(1)}, u32[]{:S(2)}, u32[]{:S(2)}) async-start(bf16[32,272,128]{2,1,0:T(8,128)(2,1)} %copy-done.4), calls=%async_computation.1 | async-start | bytes 4456448 | tf_op jit(solution)/shard_map/all_to_all | solution.py:360
  109.4 2.2 %copy-start.2 = (bf16[128,1,128,128]{3,2,1,0:T(8,128)(2,1)S(1)}, bf16[128,1,128,128]{3,2,1,0:T(8,128)(2,1)}, u32[]{:S(2)}) copy-start(bf16[128,1,128,128]{3,2,1,0:T(8,128)(2,1)} %param.13) | copy-start | bytes 12582916
  111.6 2.2 %copy-start.3 = (bf16[128,1,128,128]{3,2,1,0:T(8,128)(2,1)S(1)}, bf16[128,1,128,128]{3,2,1,0:T(8,128)(2,1)}, u32[]{:S(2)}) copy-start(bf16[128,1,128,128]{3,2,1,0:T(8,128)(2,1)} %param.14) | copy-start | bytes 12582916
  123.5 1.3 copy-start.5
  124.8 0.6 copy-start.9
  138.8 1.6 %copy-start.6 = (f32[4096,128]{1,0:T(8,128)S(1)}, f32[4096,128]{1,0:T(8,128)}, u32[]{:S(2)}) copy-start(f32[4096,128]{1,0:T(8,128)} %copy-done.5) | copy-start | bytes 6291460
  140.4 0.8 copy-start.10

commit v3 on v2

--- a/solution.py
+++ b/solution.py
@@ -70,7 +70,7 @@
         ).start()
         return carry
 
-    lax.fori_loop(0, rows, one, 0, unroll=8)
+    lax.fori_loop(0, rows, one, 0, unroll=16)
     more.wait()
     load.wait()
 
@@ -223,37 +223,49 @@
     out.wait()
 
 
-def merge_kernel(cap, per_row, batch, place_ref, x_ref, tail_ref, lse_ref, out_ref, sent_ref, weight_ref):
+def merge_kernel(cap, per_row, chunks, place_ref, x_ref, lse_ref, tail_ref, out_ref, sent_ref, weight_ref, done_ref, sems):
     owners = x_ref.shape[0]
     data = cap * per_row
-    step = pl.program_id(0)
-
-    @pl.when(step == 0)
-    def _():
-        for o in range(owners):
-            sent_ref[o * cap:(o + 1) * cap, :] = x_ref[o, data:data + EXTRA, :].astype(F32)[0:cap, :]
-
+    rows = lse_ref.shape[0]
+    batch = rows // chunks
+    part = batch * per_row
+
+    def piece(ref, c):
+        return ref.at[pl.ds(c * part, part), :]
+
+    stores = [pltpu.make_async_copy(piece(done_ref, c), piece(out_ref, c), sems.at[c]) for c in range(chunks)]
+    for o in range(owners):
+        sent_ref[o * cap:(o + 1) * cap, :] = x_ref[o, data:data + EXTRA, :].astype(F32)[0:cap, :]
     mask = lane_group_mask(per_row, 128)
     lane = lax.broadcasted_iota(jnp.int32, (batch, 128), 1)
-    places = [place_ref[0, step * batch + i] for i in range(batch)]
-    lse = jnp.concatenate([sent_ref[pl.ds(p, 1), :] for p in places], axis=0)
-    terms = jnp.where(lane < 3 * per_row, lse, -lse_ref[...])
-    ahead = terms
-    for k in range(1, 4):
-        ahead = ahead + pltpu.roll(terms, k * per_row, 1)
-    weight = 1.0 / (1.0 + jnp.exp(-ahead))
-    high = weight.astype(BF16).astype(F32)
-    mid = (weight - high).astype(BF16).astype(F32)
-    weight_ref[...] = jnp.where(lane < per_row, high, jnp.where(lane < 2 * per_row, mid, jnp.where(lane < 3 * per_row, weight - high - mid, 0.0)))
     ones = jnp.ones((128, 128), BF16)
-    for i in range(batch):
-        place = places[i]
-        spread = jnp.where(mask, weight_ref[i:i + 1, :], 0.0).astype(BF16)
+    for c in range(chunks):
+        places = [place_ref[0, c * batch + i] for i in range(batch)]
+        lse = jnp.concatenate([sent_ref[pl.ds(p, 1), :] for p in places], axis=0)
+        terms = jnp.where(lane < 3 * per_row, lse, -lse_ref[c * batch:(c + 1) * batch, :])
+        ahead = terms
+        for k in range(1, 4):
+            ahead = ahead + pltpu.roll(terms, k * per_row, 1)
+        weight = 1.0 / (1.0 + jnp.exp(-ahead))
+        high = weight.astype(BF16).astype(F32)
+        rest = weight - high
+        mid = rest.astype(BF16).astype(F32)
+        low = jnp.where(lane < 3 * per_row, rest - mid, 0.0)
+        weight_ref[c * batch:(c + 1) * batch, :] = jnp.where(lane < per_row, high, jnp.where(lane < 2 * per_row, mid, low))
+        spread = jnp.concatenate(
+            [jnp.where(mask, weight_ref[c * batch + i:c * batch + i + 1, :], 0.0).astype(BF16) for i in range(batch)], axis=0
+        )
         weight_p = jnp.dot(spread, ones, preferred_element_type=F32)
-        start = pl.multiple_of((place & 7) * per_row, per_row)
-        prefix = x_ref[lax.shift_right_logical(place, 3), pl.ds(start, per_row), :].astype(F32)
-        tail = tail_ref[i * per_row:(i + 1) * per_row, :]
-        out_ref[i * per_row:(i + 1) * per_row, :] = (tail + weight_p * (prefix - tail)).astype(BF16)
+        for i in range(batch):
+            here = slice(i * per_row, (i + 1) * per_row)
+            there = slice(c * part + i * per_row, c * part + (i + 1) * per_row)
+            start = pl.multiple_of((places[i] & 7) * per_row, per_row)
+            prefix = x_ref[lax.shift_right_logical(places[i], 3), pl.ds(start, per_row), :].astype(F32)
+            tail = tail_ref[there, :]
+            done_ref[there, :] = (tail + weight_p[here] * (prefix - tail)).astype(BF16)
+        stores[c].start()
+    for store in stores:
+        store.wait()
 
 
 def vmem():
@@ -262,6 +274,14 @@
 
 def hbm():
     return pl.BlockSpec(memory_space=pltpu.MemorySpace.HBM)
+
+
+def in_vmem(x):
+    return pltpu.with_memory_space_constraint(x, pltpu.VMEM)
+
+
+def in_hbm(x):
+    return pltpu.with_memory_space_constraint(x, pltpu.HBM)
 
 
 def smem():
@@ -288,7 +308,7 @@
     sent, place = pl.pallas_call(
         functools.partial(pack_kernel, cap, per_row),
         out_shape=(
-            jax.ShapeDtypeStruct((owners, block, width), BF16),
+            pltpu.HBM((owners, block, width), BF16),
             jax.ShapeDtypeStruct((1, rows), jnp.int32),
         ),
         in_specs=[vmem(), hbm()],
@@ -302,7 +322,7 @@
         compiler_params=params(),
         cost_estimate=pl.CostEstimate(flops=0, bytes_accessed=3 * MIB, transcendentals=0),
         name="pack",
-    )(codes, flat)
+    )(codes, in_hbm(flat))
     arrived = lax.all_to_all(sent, "roll", split_axis=0, concat_axis=0, tiled=True)
 
     batch = 8
@@ -310,8 +330,8 @@
     tail_out, tail_lse = pl.pallas_call(
         functools.partial(tail_kernel, steps, per_row, batch, scale),
         out_shape=(
-            jax.ShapeDtypeStruct((rows * per_row, width), F32),
-            jax.ShapeDtypeStruct((rows, 128), F32),
+            pltpu.VMEM((rows * per_row, width), F32),
+            pltpu.VMEM((rows, 128), F32),
         ),
         grid=(rows // batch,),
         in_specs=[
@@ -332,13 +352,13 @@
         ),
         name="tail",
     )(
-        codes, flat, tail_keys.reshape(rows * slots, width), tail_values.reshape(rows * slots, width),
+        codes, in_hbm(flat), in_hbm(tail_keys.reshape(rows * slots, width)), in_hbm(tail_values.reshape(rows * slots, width)),
         new_keys.reshape(rows * steps, width), new_values.reshape(rows * steps, width),
     )
 
     answered = pl.pallas_call(
         functools.partial(prefix_kernel, cap, per_row, pref, scale),
-        out_shape=jax.ShapeDtypeStruct((owners, block, width), BF16),
+        out_shape=pltpu.HBM((owners, block, width), BF16),
         in_specs=[vmem(), vmem(), vmem()],
         out_specs=hbm(),
         scratch_shapes=[
@@ -359,24 +379,22 @@
     )(arrived, prefix_keys.reshape(groups * pref, width), prefix_values.reshape(groups * pref, width))
     back = lax.all_to_all(answered, "roll", split_axis=0, concat_axis=0, tiled=True)
 
-    batch = 32
-    part = batch * per_row
+    chunks = 4
     merged = pl.pallas_call(
-        functools.partial(merge_kernel, cap, per_row, batch),
-        out_shape=jax.ShapeDtypeStruct((rows * per_row, width), BF16),
-        grid=(rows // batch,),
-        in_specs=[
-            smem(),
-            pl.BlockSpec((owners, block, width), lambda i: (0, 0, 0)),
-            pl.BlockSpec((part, width), lambda i: (i, 0)),
-            pl.BlockSpec((batch, 128), lambda i: (i, 0)),
+        functools.partial(merge_kernel, cap, per_row, chunks),
+        out_shape=pltpu.HBM((rows * per_row, width), BF16),
+        in_specs=[smem(), vmem(), vmem(), vmem()],
+        out_specs=hbm(),
+        scratch_shapes=[
+            pltpu.VMEM((owners * cap, 128), F32),
+            pltpu.VMEM((rows, 128), F32),
+            pltpu.VMEM((rows * per_row, width), BF16),
+            pltpu.SemaphoreType.DMA((chunks,)),
         ],
-        out_specs=pl.BlockSpec((part, width), lambda i: (i, 0)),
-        scratch_shapes=[pltpu.VMEM((owners * cap, 128), F32), pltpu.VMEM((batch, 128), F32)],
         compiler_params=params(),
         cost_estimate=pl.CostEstimate(flops=0, bytes_accessed=6 * MIB, transcendentals=0),
         name="merge",
-    )(place, back, tail_out, tail_lse)
+    )(place, in_vmem(back), in_vmem(tail_lse), in_vmem(tail_out))
     return merged.reshape(rows, steps, heads, width)
 
 

time: 144 us -> 141 us (0.979); the launches traced: 145 us -> 140 us
  local copies, waits for them, and re-layouts: 11.3 us -> 2.93 us
  Pallas kernels: 36.4 us -> 40.9 us
  starting transfers between devices: 25.1 us -> 22.4 us
  waiting for transfers between devices: 13.4 us -> 15 us
    unnamed x26 -> x12, local copies, waits for them, and re-layouts: 11.3 us -> 2.93 us
    pallas_call x1, Pallas kernels: 9.63 us -> 13.6 us  [body(): pl.pallas_call(functools.partial(tail_kernel, steps, per_row, batch, scal...]
    all_to_all x1, starting transfers between devices: 25.1 us -> 22.4 us  [body(): lax.all_to_all(answered, 'roll', split_axis=0, concat_axis=0, tiled=True)]
    pallas_call x1, Pallas kernels: 20.2 us -> 22.8 us  [body(): pl.pallas_call(functools.partial(prefix_kernel, cap, per_row, pref, scale...]
    pallas_call x2, Pallas kernels: 6.55 us -> 4.5 us  [the longest x1 2.46 us: body(): pl.pallas_call(functools.partial(pack_kernel, cap, per_row), out_shape=(p...]
    all_to_all x1, waiting for transfers between devices: 13.4 us -> 15 us  [body(): lax.all_to_all(answered, 'roll', split_axis=0, concat_axis=0, tiled=True)]
  transfers between devices with their start and end apart: 1 -> 1, of which waited for: 1 -> 1; matrix products, arithmetic and copies ran while one was open for 0% -> 0% of each run, Pallas kernels for 7% -> 10%
where the time goes in v3:
time: 141 us; the launch traced here: 140 us
  blocking collectives  57.9 us (41%)
  Pallas kernels  40.9 us (29%)
  starting transfers between devices  22.4 us (16%)
  waiting for transfers between devices  15 us (11%)
  local copies, waits for them, and re-layouts  2.93 us (2%)
    all_to_all x1, blocking collectives, body(): lax.all_to_all(sent, 'roll', split_axis=0, concat_axis=0, tiled=True)  41.8 us
    pallas_call x1, Pallas kernels, body(): pl.pallas_call(functools.partial(prefix_kernel, cap, per_row, pref, scale...  22.8 us
    all_to_all x1, starting transfers between devices, body(): lax.all_to_all(answered, 'roll', split_axis=0, concat_axis=0, tiled=True)  22.4 us
    all_gather x1, blocking collectives, body(): codes = lax.all_gather(code, 'tp', axis=0, tiled=True)  16.1 us
    all_to_all x1, waiting for transfers between devices, body(): lax.all_to_all(answered, 'roll', split_axis=0, concat_axis=0, tiled=True)  15 us
    pallas_call x1, Pallas kernels, body(): pl.pallas_call(functools.partial(tail_kernel, steps, per_row, batch, scal...  13.6 us
    unnamed x12, local copies, waits for them, and re-layouts  2.93 us
  transfers between devices with their start and end apart: 1, of which 1 were waited for; matrix products, arithmetic and copies ran while one was open for 0% of the time, Pallas kernels for 10%

profile of v3, /device:TPU:1, one launch (start us, length us, event | category | flops | bytes accessed | tf_op | source)
XLA Modules:
  0.0 140.0 jit_solution(3635367269780602163)
XLA Ops:
  0.0 0.7 add_bitcast_fusion
  0.7 16.1 %all-gather = s32[8,1,16]{2,1,0:T(1,128)S(1)} all-gather(s32[1,1,16]{2,1,0:T(1,128)S(1)} %add_bitcast_fusion), channel_id=1, replica_groups=mesh['roll'=32,'tp'=8] {'tp'}, dimensions={0}, use_global_device_ids=true | all-gather | bytes 576 | tf_op jit(solution)/shard_map/all_gather | solution.py:304
  16.8 2.5 %pack.1 = (bf16[32,272,128]{2,1,0:T(8,128)(2,1)}, s32[1,128]{1,0:T(1,128)S(1)}) custom-call(s32[8,16]{1,0:T(8,128)S(1)} %bitcast.13, bf16[4096,128]{1,0:T(8,128)(2,1)} %bitcast.17), custom_call_target="tpu_custom_call" | custom-call | bytes 3145728 | tf_op jit(solution)/shard_map/pack/pallas_call | solution.py:308
  19.3 0.0 copy-start.4
  19.3 0.0 copy-start.5
  19.3 41.8 %all_to_all.10.x_ref = bf16[32,272,128]{2,1,0:T(8,128)(2,1)S(1)} all-to-all(bf16[32,272,128]{2,1,0:T(8,128)(2,1)} %get-tuple-element.10), channel_id=1, replica_groups=mesh['roll'=32,'tp'=8] {'roll'}, dimensions={0} | all-to-all | bytes 4456448 | tf_op jit(solution)/shard_map/all_to_all | solution.py:326
  61.1 0.0 copy-done.4
  61.1 0.0 copy-done.5
  61.1 22.8 %prefix.1 = bf16[32,272,128]{2,1,0:T(8,128)(2,1)} custom-call(bf16[32,272,128]{2,1,0:T(8,128)(2,1)S(1)} %all_to_all.10.x_ref, bf16[2048,128]{1,0:T(8,128)(2,1)S(1)} %bitcast.15, bf16[2048,128]{1,0:T(8,128)(2,1)S(1)} %bitcast.16), custom_call_target="tpu_custom_call" | custom-call | flops 4294967296 | bytes 6291456 | tf_op jit(solution)/shard_map/prefix/pallas_call | solution.py:359
  83.9 0.0 copy-start.2
  83.9 0.0 copy-start.3
  83.9 22.4 %all-to-all-start.1 = ((bf16[32,272,128]{2,1,0:T(8,128)(2,1)}), bf16[32,272,128]{2,1,0:T(8,128)(2,1)S(1)}, u32[]{:S(2)}, u32[]{:S(2)}) async-start(bf16[32,272,128]{2,1,0:T(8,128)(2,1)} %prefix.1), calls=%async_computation.1 | async-start | bytes 4456448 | tf_op jit(solution)/shard_map/all_to_all | solution.py:380
  106.3 0.0 copy-done.2
  106.4 0.0 copy-done.3
  106.4 13.6 %tail.1 = (f32[4096,128]{1,0:T(8,128)S(1)}, f32[128,128]{1,0:T(8,128)S(1)}) custom-call(s32[8,16]{1,0:T(8,128)S(1)} %bitcast.14, bf16[4096,128]{1,0:T(8,128)(2,1)} %bitcast.18, bf16[16384,128]{1,0:T(8,128)(2,1)} %bitcast.19, bf16[16384,128]{1,0:T(8,128)(2,1)} %bitcast.20, bf16[512,128]{1,0:T(8,128)(2,1)S(1)} %bitcast.11, bf16[512,128]{1,0:T(8,128)(2,1)S(1)} %bitcast.12), custom_call_target="tpu_custom_call" | custom-call | flops 268435456 | bytes 12582912 | tf_op jit(solution)/shard_map/tail/pallas_call | solution.py:330
  120.0 0.0 copy-start
  120.0 1.3 copy-done
  121.3 15.0 %all-to-all-done.1.x_ref = bf16[32,272,128]{2,1,0:T(8,128)(2,1)S(1)} async-done(((bf16[32,272,128]{2,1,0:T(8,128)(2,1)}), bf16[32,272,128]{2,1,0:T(8,128)(2,1)S(1)}, u32[]{:S(2)}, u32[]{:S(2)}) %all-to-all-start.1) | async-done | bytes 2228256 | tf_op jit(solution)/shard_map/all_to_all | solution.py:380
  136.3 0.0 copy-start.1
  136.3 1.6 %copy-done.1 = f32[4096,128]{1,0:T(8,128)S(1)} copy-done((f32[4096,128]{1,0:T(8,128)S(1)}, f32[4096,128]{1,0:T(8,128)}, u32[]{:S(2)}) %copy-start.1) | copy-done | bytes 2097176
  137.9 2.0 %merge.1 = bf16[4096,128]{1,0:T(8,128)(2,1)} custom-call(s32[1,128]{1,0:T(1,128)S(1)} %get-tuple-element.9.place_ref, bf16[32,272,128]{2,1,0:T(8,128)(2,1)S(1)} %all-to-all-done.1.x_ref, f32[128,128]{1,0:T(8,128)S(1)} %get-tuple-element.11.lse_ref, f32[4096,128]{1,0:T(8,128)S(1)} %copy-done.1), custom_call_target="tpu_custom_call" | custom-call | bytes 6291456 | tf_op jit(solution)/shard_map/merge/pallas_call | solution.py:383
Async XLA Ops:
  19.3 41.8 %copy-start.4 = (bf16[2,1,1024,128]{3,2,1,0:T(8,128)(2,1)S(1)}, bf16[2,1,1024,128]{3,2,1,0:T(8,128)(2,1)}, u32[]{:S(2)}) copy-start(bf16[2,1,1024,128]{3,2,1,0:T(8,128)(2,1)} %param.15) | copy-start | bytes 1572868
  19.3 41.8 %copy-start.5 = (bf16[2,1,1024,128]{3,2,1,0:T(8,128)(2,1)S(1)}, bf16[2,1,1024,128]{3,2,1,0:T(8,128)(2,1)}, u32[]{:S(2)}) copy-start(bf16[2,1,1024,128]{3,2,1,0:T(8,128)(2,1)} %param.16) | copy-start | bytes 1572868
  83.9 22.5 %copy-start.2 = (bf16[128,4,1,128]{3,1,2,0:T(4,128)(2,1)S(1)}, bf16[128,4,1,128]{3,1,2,0:T(4,128)(2,1)}, u32[]{:S(2)}) copy-start(bf16[128,4,1,128]{3,1,2,0:T(4,128)(2,1)} %param.11) | copy-start | bytes 393220
  83.9 22.5 %copy-start.3 = (bf16[128,4,1,128]{3,1,2,0:T(4,128)(2,1)S(1)}, bf16[128,4,1,128]{3,1,2,0:T(4,128)(2,1)}, u32[]{:S(2)}) copy-start(bf16[128,4,1,128]{3,1,2,0:T(4,128)(2,1)} %param.12) | copy-start | bytes 393220
  83.9 52.4 %all-to-all-start.1 = ((bf16[32,272,128]{2,1,0:T(8,128)(2,1)}), bf16[32,272,128]{2,1,0:T(8,128)(2,1)S(1)}, u32[]{:S(2)}, u32[]{:S(2)}) async-start(bf16[32,272,128]{2,1,0:T(8,128)(2,1)} %prefix.1), calls=%async_computation.1 | async-start | bytes 4456448 | tf_op jit(solution)/shard_map/all_to_all | solution.py:380
  120.0 1.3 copy-start
  136.3 1.6 %copy-start.1 = (f32[4096,128]{1,0:T(8,128)S(1)}, f32[4096,128]{1,0:T(8,128)}, u32[]{:S(2)}) copy-start(f32[4096,128]{1,0:T(8,128)} %copy-done) | copy-start | bytes 6291460

commit v4 on v3

--- a/solution.py
+++ b/solution.py
@@ -41,21 +41,28 @@
     jl = lax.broadcasted_iota(jnp.int32, (rows, line), 1)
     picked = jnp.where(rl % line == jl, picked, 0.0).astype(BF16)
     down = jnp.dot(picked, jnp.ones((line, rows), BF16), preferred_element_type=F32)
-    earlier = lax.broadcasted_iota(jnp.int32, (rows, rows), 0) < lax.broadcasted_iota(jnp.int32, (rows, rows), 1)
-    rank = jnp.sum(jnp.where((down == across) & earlier, 1.0, 0.0), axis=0, keepdims=True).astype(jnp.int32)
-    whole = across.astype(jnp.int32)
-    slot = jnp.where((whole & 1) == 1, cap - 1 - rank, rank)
-    place = lax.shift_right_logical(whole, 1) * cap + slot
+    across = across.astype(jnp.int32)
+    down = down.astype(jnp.int32)
+    sub = lax.broadcasted_iota(jnp.int32, (rows, rows), 0)
+    lane = lax.broadcasted_iota(jnp.int32, (rows, rows), 1)
+    chip = lax.shift_right_logical(across, 2)
+    shared = lax.shift_right_logical(down, 2) == chip
+    before = shared & (down * rows + sub < across * rows + lane)
+    rank = jnp.sum(jnp.where(before, 1.0, 0.0), axis=0, keepdims=True).astype(jnp.int32)
+    number = jnp.sum(jnp.where(shared, 1.0, 0.0), axis=0, keepdims=True).astype(jnp.int32)
+    half = lax.shift_right_logical(number + 1, 1)
+    core = (rank >= half).astype(jnp.int32)
+    device = chip * 2 + core
+    place = device * cap + rank - core * half
     place_ref[...] = place
     index = pltpu.make_async_copy(place_ref, where_ref, sems.at[1])
     index.start()
-    named = lax.broadcasted_iota(jnp.int32, (2 * owners, rows), 0).astype(F32) == across
-    counts = jnp.dot(named.astype(BF16), jnp.ones((rows, 128), BF16), preferred_element_type=F32)
-    half = EXTRA // 2
-    for o in range(owners):
-        first = jnp.broadcast_to(counts[2 * o:2 * o + 1, :], (half, 128))
-        second = jnp.broadcast_to(counts[2 * o + 1:2 * o + 2, :], (half, 128))
-        extra_ref[o] = jnp.concatenate([first, second], axis=0).astype(BF16)
+    named = lax.broadcasted_iota(jnp.int32, (4 * owners, rows), 0) == device * 4 + (across & 3)
+    counts = jnp.dot(named.astype(BF16), jnp.ones((rows, 128), BF16), preferred_element_type=F32).astype(BF16)
+    ii = lax.broadcasted_iota(jnp.int32, (owners * EXTRA, 4 * owners), 0)
+    kk = lax.broadcasted_iota(jnp.int32, (owners * EXTRA, 4 * owners), 1)
+    repeat = (lax.shift_right_logical(ii, 2) == kk).astype(BF16)
+    extra_ref[...] = jnp.dot(repeat, counts, preferred_element_type=F32).astype(BF16).reshape(owners, EXTRA, 128)
     more = pltpu.make_async_copy(extra_ref, out_ref.at[:, pl.ds(cap * per_row, EXTRA), :], sems.at[2])
     more.start()
     index.wait()
@@ -121,61 +128,70 @@
 
 
 def prefix_kernel(
-    cap, per_row, pref, scale, x_ref, k_ref, v_ref, out_ref, held_ref, wide_ref, list_ref, lse_ref, sent_ref, where_ref, sems
+    cap, per_row, pref, scale, x_ref, k_ref, v_ref, ko_ref, vo_ref, out_ref, key_ref, wide_ref, list_ref, lse_ref,
+    where_ref, sems
 ):
     sources = x_ref.shape[0]
     data = cap * per_row
-    groups = v_ref.shape[0] // pref
-    half = EXTRA // 2
+    own_rows = k_ref.shape[0]
     i = lax.broadcasted_iota(jnp.int32, (sources, sources), 0)
     j = lax.broadcasted_iota(jnp.int32, (sources, sources), 1)
     lower = (j <= i).astype(BF16)
-    lane = lax.broadcasted_iota(jnp.int32, (1, 128), 1)
-    entries = []
-    totals = []
-    for g in range(2):
-        count = jnp.concatenate(
-            [x_ref[s, data:data + EXTRA, :].astype(F32)[g * half:g * half + 1, :] for s in range(sources)], axis=0
-        )
+    source = lax.broadcasted_iota(jnp.int32, (sources, 128), 0).astype(F32)
+    lane = lax.broadcasted_iota(jnp.int32, (1, 128), 1).astype(F32)
+    tiles = [x_ref[s, data:data + EXTRA, :].astype(F32) for s in range(sources)]
+    fore = jnp.zeros((sources, 128), F32)
+    end = jnp.zeros((1, 128), F32)
+    tables = []
+    for g in range(4):
+        count = jnp.concatenate([tile[4 * g:4 * g + 1, :] for tile in tiles], axis=0)
         ends = jnp.dot(lower, count.astype(BF16), preferred_element_type=F32)
         total = ends[sources - 1:sources, :]
-        totals.append(total)
-        for h in range(2):
-            at = jnp.maximum(jnp.minimum((lane + 128 * h).astype(F32), total - 1.0), 0.0)
-            passed = ends <= at
-            source = jnp.sum(jnp.where(passed, 1.0, 0.0), axis=0, keepdims=True)
-            within = at - jnp.sum(jnp.where(passed, count, 0.0), axis=0, keepdims=True)
-            entries.append(source * cap + (within if g == 0 else (cap - 1) - within))
-    list_ref[...] = jnp.concatenate(entries + totals + totals, axis=0).astype(jnp.int32)
+        tables.append((end, total, ends - count, ends, source * cap + fore))
+        fore = fore + count
+        end = end + jnp.floor((total + 7.0) * 0.125) * 8.0
+    lists = []
+    for h in range(3):
+        p = jnp.minimum(lane + 128.0 * h, end - 1.0)
+        entry = jnp.zeros((1, 128), F32)
+        for g, (base, total, begins, ends, first) in enumerate(tables):
+            at = jnp.maximum(jnp.minimum(p - base, total - 1.0), 0.0)
+            mine = (begins <= at) & (at < ends)
+            slot = jnp.sum(jnp.where(mine, first + at - begins, 0.0), axis=0, keepdims=True)
+            entry = jnp.where((p >= base) & (total > 0.0), slot + 256.0 * g, entry)
+        lists.append(entry)
+    list_ref[...] = jnp.concatenate(lists + [end] + lists + [end], axis=0).astype(jnp.int32)
     copy = pltpu.make_async_copy(list_ref, where_ref, sems.at[0])
     copy.start()
-    wide_ref[:, 0:128] = v_ref[...]
-    wide_ref[:, 128:256] = jnp.ones((groups * pref, 128), BF16)
+    core = lax.axis_index("roll") & 1
+    mine = pl.ds(pl.multiple_of(core * own_rows, own_rows), own_rows)
+    other = pl.ds(pl.multiple_of((1 - core) * own_rows, own_rows), own_rows)
+    key_ref[mine, :] = k_ref[...]
+    key_ref[other, :] = ko_ref[...]
+    wide_ref[mine, 0:128] = v_ref[...]
+    wide_ref[other, 0:128] = vo_ref[...]
+    wide_ref[:, 128:256] = jnp.ones((2 * own_rows, 128), BF16)
     lse_ref[...] = jnp.zeros(lse_ref.shape, F32)
     copy.wait()
-    found = [where_ref[4, 0], where_ref[5, 0]]
+    found = where_ref[3, 0]
     mask = lane_group_mask(per_row, 128)
     factor = scale * LOG2E
 
     def attend(unit, sub, shifted):
-        first_units = (found[0] + unit - 1) // unit
-        units = first_units + (found[1] + unit - 1) // unit
-
         def one(b, carry):
-            g = (b >= first_units).astype(jnp.int32)
-            j = (b - g * first_units) * unit
-            row = 2 * g + lax.shift_right_logical(j, 7)
-            first = j & 127
-            slots = [where_ref[row, first + i] for i in range(unit)]
+            row = lax.shift_right_logical(b * unit, 7)
+            first = (b * unit) & 127
+            entries = [where_ref[row, first + i] for i in range(unit)]
+            slots = [e & 255 for e in entries]
             own = [lax.shift_right_logical(s, 3) for s in slots]
             start = [pl.multiple_of((s & 7) * per_row, per_row) for s in slots]
-            here = pl.multiple_of(g * pref, pref)
+            here = [pl.multiple_of(lax.shift_right_logical(entries[t], 8) * pref, pref) for t in range(0, unit, sub)]
             scores = []
             for t in range(0, unit, sub):
                 q = jnp.concatenate([x_ref[own[i], pl.ds(start[i], per_row), :] for i in range(t, t + sub)], axis=0)
                 scores.append(
                     lax.dot_general(
-                        q, k_ref[pl.ds(here, pref), :], (((1,), (1,)), ((), ())), preferred_element_type=F32
+                        q, key_ref[pl.ds(here[t // sub], pref), :], (((1,), (1,)), ((), ())), preferred_element_type=F32
                     )
                 )
             low, high = carry
@@ -183,7 +199,7 @@
                 score = scores[t // sub]
                 top = jnp.max(score, axis=1, keepdims=True) if shifted else None
                 expo = jnp.exp2((score - top if shifted else score) * factor).astype(BF16)
-                both = jnp.dot(expo, wide_ref[pl.ds(here, pref), :], preferred_element_type=F32)
+                both = jnp.dot(expo, wide_ref[pl.ds(here[t // sub], pref), :], preferred_element_type=F32)
                 total = both[:, 128:256]
                 result = (both[:, 0:128] / total).astype(BF16)
                 lse = jnp.log(total)
@@ -194,13 +210,13 @@
                 high = jnp.maximum(high, jnp.max(stacked, axis=0))
                 for i in range(sub):
                     part = slice(i * per_row, (i + 1) * per_row)
-                    held_ref[own[t + i], pl.ds(start[t + i], per_row), :] = result[part]
+                    out_ref[own[t + i], pl.ds(start[t + i], per_row), :] = result[part]
                     lse_ref[pl.ds(slots[t + i], 1), :] = jnp.sum(
                         jnp.where(mask, lse[part], 0.0), axis=0, keepdims=True
                     )
             return low, high
 
-        return lax.fori_loop(0, units, one, (jnp.ones((8, 128), F32), jnp.ones((8, 128), F32)))
+        return lax.fori_loop(0, (found + unit - 1) // unit, one, (jnp.ones((8, 128), F32), jnp.ones((8, 128), F32)))
 
     low, high = attend(32, 8, False)
     safe = (jnp.min(low) > 2.0**-70) & (jnp.max(high) < 2.0**100)
@@ -217,10 +233,7 @@
         low_part = rest - mid_part
         lanes = lax.broadcasted_iota(jnp.int32, full.shape, 1)
         sent = jnp.where(lanes < per_row, high_part, jnp.where(lanes < 2 * per_row, mid_part, low_part))
-        held_ref[s, data:data + EXTRA, :] = jnp.concatenate([sent, jnp.zeros_like(sent)], axis=0).astype(BF16)
-    out = pltpu.make_async_copy(held_ref, out_ref, sems.at[0])
-    out.start()
-    out.wait()
+        out_ref[s, data:data + EXTRA, :] = jnp.concatenate([sent, jnp.zeros_like(sent)], axis=0).astype(BF16)
 
 
 def merge_kernel(cap, per_row, chunks, place_ref, x_ref, lse_ref, tail_ref, out_ref, sent_ref, weight_ref, done_ref, sems):
@@ -303,7 +316,9 @@
     code = (route_owner * 2 + group_slot) * 256 + tail_len
     codes = lax.all_gather(code, "tp", axis=0, tiled=True)
     flat = queries.reshape(rows * per_row, width)
-    params = functools.partial(pltpu.CompilerParams, vmem_limit_bytes=32 * MIB)
+
+    def params(grant):
+        return pltpu.CompilerParams(vmem_limit_bytes=grant * MIB)
 
     sent, place = pl.pallas_call(
         functools.partial(pack_kernel, cap, per_row),
@@ -319,7 +334,7 @@
             pltpu.SMEM((1, rows), jnp.int32),
             pltpu.SemaphoreType.DMA((3,)),
         ],
-        compiler_params=params(),
+        compiler_params=params(8),
         cost_estimate=pl.CostEstimate(flops=0, bytes_accessed=3 * MIB, transcendentals=0),
         name="pack",
     )(codes, in_hbm(flat))
@@ -346,7 +361,7 @@
             pl.BlockSpec((part, width), lambda i: (i, 0)),
             pl.BlockSpec((batch, 128), lambda i: (i, 0)),
         ),
-        compiler_params=params(),
+        compiler_params=params(16),
         cost_estimate=pl.CostEstimate(
             flops=4 * rows * per_row * slots * width, bytes_accessed=12 * MIB, transcendentals=rows * per_row * slots
         ),
@@ -356,27 +371,32 @@
         new_keys.reshape(rows * steps, width), new_values.reshape(rows * steps, width),
     )
 
+    keys = prefix_keys.reshape(groups * pref, width)
+    values = prefix_values.reshape(groups * pref, width)
+    pairs = [(i, i ^ 1) for i in range(owners)]
+    keys_other = lax.ppermute(keys, "roll", pairs)
+    values_other = lax.ppermute(values, "roll", pairs)
+    arrived, tail_out, tail_lse = lax.optimization_barrier((arrived, tail_out, tail_lse))
     answered = pl.pallas_call(
         functools.partial(prefix_kernel, cap, per_row, pref, scale),
-        out_shape=pltpu.HBM((owners, block, width), BF16),
-        in_specs=[vmem(), vmem(), vmem()],
-        out_specs=hbm(),
+        out_shape=pltpu.VMEM((owners, block, width), BF16),
+        in_specs=[vmem()] * 5,
+        out_specs=vmem(),
         scratch_shapes=[
-            pltpu.VMEM((owners, block, width), BF16),
-            pltpu.VMEM((groups * pref, 2 * width), BF16),
+            pltpu.VMEM((2 * groups * pref, width), BF16),
+            pltpu.VMEM((2 * groups * pref, 2 * width), BF16),
             pltpu.VMEM((8, 128), jnp.int32),
-            pltpu.VMEM((owners * cap, 128), F32),
             pltpu.VMEM((owners * cap, 128), F32),
             pltpu.SMEM((8, 128), jnp.int32),
             pltpu.SemaphoreType.DMA((1,)),
         ],
-        compiler_params=params(),
+        compiler_params=params(24),
         cost_estimate=pl.CostEstimate(
             flops=4 * owners * cap * per_row * pref * width, bytes_accessed=6 * MIB,
             transcendentals=owners * cap * per_row * pref,
         ),
         name="prefix",
-    )(arrived, prefix_keys.reshape(groups * pref, width), prefix_values.reshape(groups * pref, width))
+    )(arrived, keys, values, keys_other, values_other)
     back = lax.all_to_all(answered, "roll", split_axis=0, concat_axis=0, tiled=True)
 
     chunks = 4
@@ -391,7 +411,7 @@
             pltpu.VMEM((rows * per_row, width), BF16),
             pltpu.SemaphoreType.DMA((chunks,)),
         ],
-        compiler_params=params(),
+        compiler_params=params(12),
         cost_estimate=pl.CostEstimate(flops=0, bytes_accessed=6 * MIB, transcendentals=0),
         name="merge",
     )(place, in_vmem(back), in_vmem(tail_lse), in_vmem(tail_out))

time: 141 us -> 130 us (0.922)
  starting transfers between devices: 22.4 us -> 12.3 us
  local copies, waits for them, and re-layouts: 2.93 us -> 1.34 us
    all_to_all x1, starting transfers between devices: 22.4 us -> 11.7 us  [body(): lax.all_to_all(sent, 'roll', split_axis=0, concat_axis=0, tiled=True)]
    unnamed x12 -> x10, local copies, waits for them, and re-layouts: 2.93 us -> 1.34 us
  transfers between devices with their start and end apart: 1 -> 3, of which waited for: 1 -> 1; matrix products, arithmetic and copies ran while one was open for 0% -> 0% of each run, Pallas kernels for 10% -> 11%
where the time goes in v4:
time: 130 us; the launch traced here: 128 us
  blocking collectives  58.5 us (45%)
  Pallas kernels  41.4 us (32%)
  waiting for transfers between devices  13.7 us (11%)
  starting transfers between devices  12.3 us (9%)
  local copies, waits for them, and re-layouts  1.34 us (1%)
    all_to_all x1, blocking collectives, body(): lax.all_to_all(answered, 'roll', split_axis=0, concat_axis=0, tiled=True)  42.4 us
    pallas_call x1, Pallas kernels, body(): pl.pallas_call(functools.partial(prefix_kernel, cap, per_row, pref, scale...  23.4 us
    all_gather x1, blocking collectives, body(): codes = lax.all_gather(code, 'tp', axis=0, tiled=True)  16.1 us
    all_to_all x1, waiting for transfers between devices, body(): lax.all_to_all(sent, 'roll', split_axis=0, concat_axis=0, tiled=True)  13.7 us
    pallas_call x1, Pallas kernels, body(): pl.pallas_call(functools.partial(tail_kernel, steps, per_row, batch, scal...  13.6 us
    all_to_all x1, starting transfers between devices, body(): lax.all_to_all(sent, 'roll', split_axis=0, concat_axis=0, tiled=True)  11.7 us
  transfers between devices with their start and end apart: 3, of which 1 were waited for; matrix products, arithmetic and copies ran while one was open for 0% of the time, Pallas kernels for 11%

profile of v4, /device:TPU:1, one launch (start us, length us, event | category | flops | bytes accessed | tf_op | source)
XLA Modules:
  0.0 128.0 jit_solution(576753442562147332)
XLA Ops:
  0.0 0.7 add_bitcast_fusion
  0.7 16.1 %all-gather = s32[8,1,16]{2,1,0:T(1,128)S(1)} all-gather(s32[1,1,16]{2,1,0:T(1,128)S(1)} %add_bitcast_fusion), channel_id=1, replica_groups=mesh['roll'=32,'tp'=8] {'tp'}, dimensions={0}, use_global_device_ids=true | all-gather | bytes 576 | tf_op jit(solution)/shard_map/all_gather | solution.py:317
  16.8 2.4 %pack.1 = (bf16[32,272,128]{2,1,0:T(8,128)(2,1)}, s32[1,128]{1,0:T(1,128)S(1)}) custom-call(s32[8,16]{1,0:T(8,128)S(1)} %bitcast.13, bf16[4096,128]{1,0:T(8,128)(2,1)} %bitcast.17), custom_call_target="tpu_custom_call" | custom-call | bytes 3145728 | tf_op jit(solution)/shard_map/pack/pallas_call | solution.py:323
  19.2 0.0 copy-start.4
  19.2 0.0 copy-start.2
  19.2 0.0 copy-start.3
  19.2 11.7 %all-to-all-start = ((bf16[32,272,128]{2,1,0:T(8,128)(2,1)}), bf16[32,272,128]{2,1,0:T(8,128)(2,1)S(1)}, u32[]{:S(2)}, u32[]{:S(2)}) async-start(bf16[32,272,128]{2,1,0:T(8,128)(2,1)} %get-tuple-element.13), calls=%async_computation | async-start | bytes 4456448 | tf_op jit(solution)/shard_map/all_to_all | solution.py:341
  30.9 0.0 copy-done.4
  30.9 0.3 collective-permute-start
  31.2 0.3 collective-permute-start.1
  31.5 0.0 copy-done.2
  31.5 0.0 copy-done.3
  31.5 13.6 %tail.1 = (f32[4096,128]{1,0:T(8,128)S(1)}, f32[128,128]{1,0:T(8,128)S(1)}) custom-call(s32[8,16]{1,0:T(8,128)S(1)} %bitcast.14, bf16[4096,128]{1,0:T(8,128)(2,1)} %bitcast.18, bf16[16384,128]{1,0:T(8,128)(2,1)} %bitcast.19, bf16[16384,128]{1,0:T(8,128)(2,1)} %bitcast.20, bf16[512,128]{1,0:T(8,128)(2,1)S(1)} %bitcast.11, bf16[512,128]{1,0:T(8,128)(2,1)S(1)} %bitcast.12), custom_call_target="tpu_custom_call" | custom-call | flops 268435456 | bytes 12582912 | tf_op jit(solution)/shard_map/tail/pallas_call | solution.py:345
  45.1 0.0 copy-start
  45.1 1.3 %copy-done = f32[4096,128]{1,0:T(8,128)} copy-done((f32[4096,128]{1,0:T(8,128)}, f32[4096,128]{1,0:T(8,128)S(1)}, u32[]{:S(2)}) %copy-start) | copy-done | bytes 2097176
  46.4 13.7 %all-to-all-done.x_ref = bf16[32,272,128]{2,1,0:T(8,128)(2,1)S(1)} async-done(((bf16[32,272,128]{2,1,0:T(8,128)(2,1)}), bf16[32,272,128]{2,1,0:T(8,128)(2,1)S(1)}, u32[]{:S(2)}, u32[]{:S(2)}) %all-to-all-start) | async-done | bytes 2228256 | tf_op jit(solution)/shard_map/all_to_all | solution.py:341
  60.1 0.0 collective-permute-done.ko_ref
  60.1 0.0 collective-permute-done.1.vo_ref
  60.2 23.4 %prefix.1 = bf16[32,272,128]{2,1,0:T(8,128)(2,1)S(1)} custom-call(bf16[32,272,128]{2,1,0:T(8,128)(2,1)S(1)} %all-to-all-done.x_ref, bf16[2048,128]{1,0:T(8,128)(2,1)S(1)} %bitcast.16, bf16[2048,128]{1,0:T(8,128)(2,1)} %bitcast.8.v_ref, bf16[2048,128]{1,0:T(8,128)(2,1)} %collective-permute-done.ko_ref, bf16[2048,128]{1,0:T(8,128)(2,1)} %collective-permute-done.1.vo_ref), custom_call_target="tpu_custom_call" | custom-call | flops 4294967296 | bytes 6291456 | tf_op jit(solution)/shard_map/prefix/pallas_call | solution.py:380
  83.6 0.0 copy-start.1
  83.6 42.4 %all_to_all.10.x_ref = bf16[32,272,128]{2,1,0:T(8,128)(2,1)S(1)} all-to-all(bf16[32,272,128]{2,1,0:T(8,128)(2,1)S(1)} %prefix.1), channel_id=1, replica_groups=mesh['roll'=32,'tp'=8] {'roll'}, dimensions={0} | all-to-all | bytes 4456448 | tf_op jit(solution)/shard_map/all_to_all | solution.py:400
  126.0 0.0 copy-done.1
  126.0 2.0 %merge.1 = bf16[4096,128]{1,0:T(8,128)(2,1)} custom-call(s32[1,128]{1,0:T(1,128)S(1)} %get-tuple-element.12.place_ref, bf16[32,272,128]{2,1,0:T(8,128)(2,1)S(1)} %all_to_all.10.x_ref, f32[128,128]{1,0:T(8,128)S(1)} %get-tuple-element.17.lse_ref, f32[4096,128]{1,0:T(8,128)S(1)} %copy-done.1), custom_call_target="tpu_custom_call" | custom-call | bytes 6291456 | tf_op jit(solution)/shard_map/merge/pallas_call | solution.py:403
Async XLA Ops:
  19.2 11.7 %copy-start.4 = (bf16[2,1,1024,128]{3,2,1,0:T(8,128)(2,1)S(1)}, bf16[2,1,1024,128]{3,2,1,0:T(8,128)(2,1)}, u32[]{:S(2)}) copy-start(bf16[2,1,1024,128]{3,2,1,0:T(8,128)(2,1)} %param.15) | copy-start | bytes 1572868
  19.2 12.3 %copy-start.2 = (bf16[128,4,1,128]{3,1,2,0:T(4,128)(2,1)S(1)}, bf16[128,4,1,128]{3,1,2,0:T(4,128)(2,1)}, u32[]{:S(2)}) copy-start(bf16[128,4,1,128]{3,1,2,0:T(4,128)(2,1)} %param.11) | copy-start | bytes 393220
  19.2 12.3 %copy-start.3 = (bf16[128,4,1,128]{3,1,2,0:T(4,128)(2,1)S(1)}, bf16[128,4,1,128]{3,1,2,0:T(4,128)(2,1)}, u32[]{:S(2)}) copy-start(bf16[128,4,1,128]{3,1,2,0:T(4,128)(2,1)} %param.12) | copy-start | bytes 393220
  19.2 40.9 %all-to-all-start = ((bf16[32,272,128]{2,1,0:T(8,128)(2,1)}), bf16[32,272,128]{2,1,0:T(8,128)(2,1)S(1)}, u32[]{:S(2)}, u32[]{:S(2)}) async-start(bf16[32,272,128]{2,1,0:T(8,128)(2,1)} %get-tuple-element.13), calls=%async_computation | async-start | bytes 4456448 | tf_op jit(solution)/shard_map/all_to_all | solution.py:341
  30.9 29.3 %collective-permute-start = (bf16[2048,128]{1,0:T(8,128)(2,1)S(1)}, bf16[2048,128]{1,0:T(8,128)(2,1)}, u32[]{:S(2)}, u32[]{:S(2)}) collective-permute-start(bf16[2048,128]{1,0:T(8,128)(2,1)S(1)} %bitcast.15), channel_id=1, source_target_pairs={{0,8},{8,0},{16,24},{24,16},{32,40},{40,32},{48,56},{56,48},{64,72... | collective-permute-start | bytes 1572872 | tf_op jit(solution)/shard_map/ppermute | solution.py:377
  31.2 28.9 %collective-permute-start.1 = (bf16[2048,128]{1,0:T(8,128)(2,1)}, bf16[2048,128]{1,0:T(8,128)(2,1)}, u32[]{:S(2)}, u32[]{:S(2)}) collective-permute-start(bf16[2048,128]{1,0:T(8,128)(2,1)} %bitcast.8.v_ref), channel_id=1, source_target_pairs={{0,8},{8,0},{16,24},{24,16},{32,40},{40,32},{48,56},{56,48},{64,72... | collective-permute-start | bytes 1572872 | tf_op jit(solution)/shard_map/ppermute | solution.py:378
  45.1 1.3 %copy-start = (f32[4096,128]{1,0:T(8,128)}, f32[4096,128]{1,0:T(8,128)S(1)}, u32[]{:S(2)}) copy-start(f32[4096,128]{1,0:T(8,128)S(1)} %get-tuple-element.18.tail_ref) | copy-start | bytes 6291460
  83.6 42.5 %copy-start.1 = (f32[4096,128]{1,0:T(8,128)S(1)}, f32[4096,128]{1,0:T(8,128)}, u32[]{:S(2)}) copy-start(f32[4096,128]{1,0:T(8,128)} %copy-done) | copy-start | bytes 6291460

commit v5 on v4

--- a/solution.py
+++ b/solution.py
@@ -12,7 +12,7 @@
 MIB = 1 << 20
 F32 = jnp.float32
 BF16 = jnp.bfloat16
-EXTRA = 16
+EXTRA = 8
 
 
 def lane_group_mask(per_row, width):
@@ -50,7 +50,7 @@
     before = shared & (down * rows + sub < across * rows + lane)
     rank = jnp.sum(jnp.where(before, 1.0, 0.0), axis=0, keepdims=True).astype(jnp.int32)
     number = jnp.sum(jnp.where(shared, 1.0, 0.0), axis=0, keepdims=True).astype(jnp.int32)
-    half = lax.shift_right_logical(number + 1, 1)
+    half = lax.shift_right_logical(number + ((lax.axis_index("roll") + chip) & 1), 1)
     core = (rank >= half).astype(jnp.int32)
     device = chip * 2 + core
     place = device * cap + rank - core * half
@@ -61,7 +61,7 @@
     counts = jnp.dot(named.astype(BF16), jnp.ones((rows, 128), BF16), preferred_element_type=F32).astype(BF16)
     ii = lax.broadcasted_iota(jnp.int32, (owners * EXTRA, 4 * owners), 0)
     kk = lax.broadcasted_iota(jnp.int32, (owners * EXTRA, 4 * owners), 1)
-    repeat = (lax.shift_right_logical(ii, 2) == kk).astype(BF16)
+    repeat = (lax.shift_right_logical(ii, 1) == kk).astype(BF16)
     extra_ref[...] = jnp.dot(repeat, counts, preferred_element_type=F32).astype(BF16).reshape(owners, EXTRA, 128)
     more = pltpu.make_async_copy(extra_ref, out_ref.at[:, pl.ds(cap * per_row, EXTRA), :], sems.at[2])
     more.start()
@@ -144,7 +144,7 @@
     end = jnp.zeros((1, 128), F32)
     tables = []
     for g in range(4):
-        count = jnp.concatenate([tile[4 * g:4 * g + 1, :] for tile in tiles], axis=0)
+        count = jnp.concatenate([tile[2 * g:2 * g + 1, :] for tile in tiles], axis=0)
         ends = jnp.dot(lower, count.astype(BF16), preferred_element_type=F32)
         total = ends[sources - 1:sources, :]
         tables.append((end, total, ends - count, ends, source * cap + fore))
@@ -177,10 +177,10 @@
     mask = lane_group_mask(per_row, 128)
     factor = scale * LOG2E
 
-    def attend(unit, sub, shifted):
+    def attend(unit, sub, shifted, begin, stop, bounds):
         def one(b, carry):
-            row = lax.shift_right_logical(b * unit, 7)
-            first = (b * unit) & 127
+            row = lax.shift_right_logical(begin + b * unit, 7)
+            first = (begin + b * unit) & 127
             entries = [where_ref[row, first + i] for i in range(unit)]
             slots = [e & 255 for e in entries]
             own = [lax.shift_right_logical(s, 3) for s in slots]
@@ -216,14 +216,17 @@
                     )
             return low, high
 
-        return lax.fori_loop(0, (found + unit - 1) // unit, one, (jnp.ones((8, 128), F32), jnp.ones((8, 128), F32)))
-
-    low, high = attend(32, 8, False)
+        return lax.fori_loop(0, lax.shift_right_logical(stop - begin + unit - 1, unit.bit_length() - 1), one, bounds)
+
+    bounds = (jnp.ones((8, 128), F32), jnp.ones((8, 128), F32))
+    most = lax.shift_left(lax.shift_right_logical(found + 8, 5), 5)
+    bounds = attend(32, 8, False, 0, most, bounds)
+    low, high = attend(16, 8, False, most, found, bounds)
     safe = (jnp.min(low) > 2.0**-70) & (jnp.max(high) < 2.0**100)
 
     @pl.when(jnp.logical_not(safe))
     def _():
-        attend(8, 8, True)
+        attend(8, 8, True, 0, found, bounds)
 
     for s in range(sources):
         full = lse_ref[s * cap:(s + 1) * cap, :]
@@ -233,7 +236,7 @@
         low_part = rest - mid_part
         lanes = lax.broadcasted_iota(jnp.int32, full.shape, 1)
         sent = jnp.where(lanes < per_row, high_part, jnp.where(lanes < 2 * per_row, mid_part, low_part))
-        out_ref[s, data:data + EXTRA, :] = jnp.concatenate([sent, jnp.zeros_like(sent)], axis=0).astype(BF16)
+        out_ref[s, data:data + EXTRA, :] = sent.astype(BF16)
 
 
 def merge_kernel(cap, per_row, chunks, place_ref, x_ref, lse_ref, tail_ref, out_ref, sent_ref, weight_ref, done_ref, sems):
@@ -314,7 +317,8 @@
     groups = prefix_keys.shape[0]
     block = cap * per_row + EXTRA
     code = (route_owner * 2 + group_slot) * 256 + tail_len
-    codes = lax.all_gather(code, "tp", axis=0, tiled=True)
+    lines = lax.axis_size("tp")
+    codes = lax.all_to_all(jnp.broadcast_to(code, (lines, code.shape[1])), "tp", split_axis=0, concat_axis=0, tiled=True)
     flat = queries.reshape(rows * per_row, width)
 
     def params(grant):

time: 130 us -> 126 us (0.969)
  starting transfers between devices: 12.3 us -> 9.92 us
    all_gather x1 -> x0, blocking collectives: 16.1 us -> none  [body(): codes = lax.all_gather(code, 'tp', axis=0, tiled=True)]
    all_to_all x0 -> x1, blocking collectives: none -> 15.3 us  [body(): lax.all_to_all(jnp.broadcast_to(code, (lines, code.shape[1])), 'tp', spli...]
    all_to_all x1, starting transfers between devices: 11.7 us -> 9.32 us  [body(): lax.all_to_all(sent, 'roll', split_axis=0, concat_axis=0, tiled=True)]
where the time goes in v5:
time: 126 us; the launch traced here: 125 us
  blocking collectives  58.1 us (46%)
  Pallas kernels  41.9 us (33%)
  waiting for transfers between devices  13 us (10%)
  starting transfers between devices  9.92 us (8%)
  local copies, waits for them, and re-layouts  1.34 us (1%)
    all_to_all x1, blocking collectives, body(): lax.all_to_all(answered, 'roll', split_axis=0, concat_axis=0, tiled=True)  42.8 us
    pallas_call x1, Pallas kernels, body(): pl.pallas_call(functools.partial(prefix_kernel, cap, per_row, pref, scale...  23.8 us
    all_to_all x1, blocking collectives, body(): lax.all_to_all(jnp.broadcast_to(code, (lines, code.shape[1])), 'tp', spli...  15.3 us
    pallas_call x1, Pallas kernels, body(): pl.pallas_call(functools.partial(tail_kernel, steps, per_row, batch, scal...  13.6 us
    all_to_all x1, waiting for transfers between devices, body(): lax.all_to_all(sent, 'roll', split_axis=0, concat_axis=0, tiled=True)  13 us
    all_to_all x1, starting transfers between devices, body(): lax.all_to_all(sent, 'roll', split_axis=0, concat_axis=0, tiled=True)  9.32 us
  transfers between devices with their start and end apart: 3, of which 1 were waited for; matrix products, arithmetic and copies ran while one was open for 0% of the time, Pallas kernels for 11%

profile of v5, /device:TPU:1, one launch (start us, length us, event | category | flops | bytes accessed | tf_op | source)
XLA Modules:
  0.0 125.1 jit_solution(10934199559123332437)
XLA Ops:
  0.0 0.7 add_bitcast_fusion
  0.7 15.3 %all_to_all.18 = s32[8,1,16]{2,1,0:T(1,128)S(1)} all-to-all(s32[8,1,16]{2,1,0:T(1,128)S(1)} %broadcast_in_dim.2), channel_id=1, replica_groups=mesh['roll'=32,'tp'=8] {'tp'}, dimensions={0} | all-to-all | bytes 1024 | tf_op jit(solution)/shard_map/all_to_all | solution.py:321
  16.0 2.4 %pack.1 = (bf16[32,264,128]{2,1,0:T(8,128)(2,1)}, s32[1,128]{1,0:T(1,128)S(1)}) custom-call(s32[8,16]{1,0:T(8,128)S(1)} %bitcast.13, bf16[4096,128]{1,0:T(8,128)(2,1)} %bitcast.19), custom_call_target="tpu_custom_call" | custom-call | bytes 3145728 | tf_op jit(solution)/shard_map/pack/pallas_call | solution.py:327
  18.4 0.0 copy-start.4
  18.4 0.0 copy-start.5
  18.5 0.0 copy-start.2
  18.5 0.0 copy-start.3
  18.5 9.3 %all-to-all-start.1 = ((bf16[32,264,128]{2,1,0:T(8,128)(2,1)}), bf16[32,264,128]{2,1,0:T(8,128)(2,1)S(1)}, u32[]{:S(2)}, u32[]{:S(2)}) async-start(bf16[32,264,128]{2,1,0:T(8,128)(2,1)} %get-tuple-element.13), calls=%async_computation.1 | async-start | bytes 4325376 | tf_op jit(solution)/shard_map/all_to_all | solution.py:345
  27.8 0.0 copy-done.4
  27.8 0.3 collective-permute-start
  28.1 0.0 copy-done.5
  28.1 0.3 collective-permute-start.1
  28.4 0.0 copy-done.2
  28.4 0.0 copy-done.3
  28.4 13.6 %tail.1 = (f32[4096,128]{1,0:T(8,128)S(1)}, f32[128,128]{1,0:T(8,128)S(1)}) custom-call(s32[8,16]{1,0:T(8,128)S(1)} %bitcast.14, bf16[4096,128]{1,0:T(8,128)(2,1)} %bitcast.20, bf16[16384,128]{1,0:T(8,128)(2,1)} %bitcast.21, bf16[16384,128]{1,0:T(8,128)(2,1)} %bitcast.22, bf16[512,128]{1,0:T(8,128)(2,1)S(1)} %bitcast.11, bf16[512,128]{1,0:T(8,128)(2,1)S(1)} %bitcast.12), custom_call_target="tpu_custom_call" | custom-call | flops 268435456 | bytes 12582912 | tf_op jit(solution)/shard_map/tail/pallas_call | solution.py:349
  42.0 0.0 copy-start
  42.1 1.3 %copy-done = f32[4096,128]{1,0:T(8,128)} copy-done((f32[4096,128]{1,0:T(8,128)}, f32[4096,128]{1,0:T(8,128)S(1)}, u32[]{:S(2)}) %copy-start) | copy-done | bytes 2097176
  43.4 13.0 %all-to-all-done.1.x_ref = bf16[32,264,128]{2,1,0:T(8,128)(2,1)S(1)} async-done(((bf16[32,264,128]{2,1,0:T(8,128)(2,1)}), bf16[32,264,128]{2,1,0:T(8,128)(2,1)S(1)}, u32[]{:S(2)}, u32[]{:S(2)}) %all-to-all-start.1) | async-done | bytes 2162720 | tf_op jit(solution)/shard_map/all_to_all | solution.py:345
  56.4 0.0 collective-permute-done.ko_ref
  56.4 0.0 collective-permute-done.1.vo_ref
  56.4 23.8 %prefix.1 = bf16[32,264,128]{2,1,0:T(8,128)(2,1)S(1)} custom-call(bf16[32,264,128]{2,1,0:T(8,128)(2,1)S(1)} %all-to-all-done.1.x_ref, bf16[2048,128]{1,0:T(8,128)(2,1)S(1)} %bitcast.16, bf16[2048,128]{1,0:T(8,128)(2,1)S(1)} %bitcast.18, bf16[2048,128]{1,0:T(8,128)(2,1)} %collective-permute-done.ko_ref, bf16[2048,128]{1,0:T(8,128)(2,1)} %collective-permute-done.1.vo_ref), custom_call_target="tpu_custom_call" | custom-call | flops 4294967296 | bytes 6291456 | tf_op jit(solution)/shard_map/prefix/pallas_call | solution.py:384
  80.2 0.0 copy-start.1
  80.2 42.8 %all_to_all.19.x_ref = bf16[32,264,128]{2,1,0:T(8,128)(2,1)S(1)} all-to-all(bf16[32,264,128]{2,1,0:T(8,128)(2,1)S(1)} %prefix.1), channel_id=1, replica_groups=mesh['roll'=32,'tp'=8] {'roll'}, dimensions={0} | all-to-all | bytes 4325376 | tf_op jit(solution)/shard_map/all_to_all | solution.py:404
  123.0 0.0 copy-done.1
  123.0 2.1 %merge.1 = bf16[4096,128]{1,0:T(8,128)(2,1)} custom-call(s32[1,128]{1,0:T(1,128)S(1)} %get-tuple-element.12.place_ref, bf16[32,264,128]{2,1,0:T(8,128)(2,1)S(1)} %all_to_all.19.x_ref, f32[128,128]{1,0:T(8,128)S(1)} %get-tuple-element.17.lse_ref, f32[4096,128]{1,0:T(8,128)S(1)} %copy-done.1), custom_call_target="tpu_custom_call" | custom-call | bytes 6291456 | tf_op jit(solution)/shard_map/merge/pallas_call | solution.py:407
  (1 shorter events, 0.0 us)
Async XLA Ops:
  18.4 9.4 %copy-start.4 = (bf16[2,1,1024,128]{3,2,1,0:T(8,128)(2,1)S(1)}, bf16[2,1,1024,128]{3,2,1,0:T(8,128)(2,1)}, u32[]{:S(2)}) copy-start(bf16[2,1,1024,128]{3,2,1,0:T(8,128)(2,1)} %param.15) | copy-start | bytes 1572868
  18.4 9.7 %copy-start.5 = (bf16[2,1,1024,128]{3,2,1,0:T(8,128)(2,1)S(1)}, bf16[2,1,1024,128]{3,2,1,0:T(8,128)(2,1)}, u32[]{:S(2)}) copy-start(bf16[2,1,1024,128]{3,2,1,0:T(8,128)(2,1)} %param.16) | copy-start | bytes 1572868
  18.5 10.0 %copy-start.2 = (bf16[128,4,1,128]{3,1,2,0:T(4,128)(2,1)S(1)}, bf16[128,4,1,128]{3,1,2,0:T(4,128)(2,1)}, u32[]{:S(2)}) copy-start(bf16[128,4,1,128]{3,1,2,0:T(4,128)(2,1)} %param.11) | copy-start | bytes 393220
  18.5 10.0 %copy-start.3 = (bf16[128,4,1,128]{3,1,2,0:T(4,128)(2,1)S(1)}, bf16[128,4,1,128]{3,1,2,0:T(4,128)(2,1)}, u32[]{:S(2)}) copy-start(bf16[128,4,1,128]{3,1,2,0:T(4,128)(2,1)} %param.12) | copy-start | bytes 393220
  18.5 37.9 %all-to-all-start.1 = ((bf16[32,264,128]{2,1,0:T(8,128)(2,1)}), bf16[32,264,128]{2,1,0:T(8,128)(2,1)S(1)}, u32[]{:S(2)}, u32[]{:S(2)}) async-start(bf16[32,264,128]{2,1,0:T(8,128)(2,1)} %get-tuple-element.13), calls=%async_computation.1 | async-start | bytes 4325376 | tf_op jit(solution)/shard_map/all_to_all | solution.py:345
  27.8 28.6 %collective-permute-start = (bf16[2048,128]{1,0:T(8,128)(2,1)S(1)}, bf16[2048,128]{1,0:T(8,128)(2,1)}, u32[]{:S(2)}, u32[]{:S(2)}) collective-permute-start(bf16[2048,128]{1,0:T(8,128)(2,1)S(1)} %bitcast.15), channel_id=1, source_target_pairs={{0,8},{8,0},{16,24},{24,16},{32,40},{40,32},{48,56},{56,48},{64,72... | collective-permute-start | bytes 1572872 | tf_op jit(solution)/shard_map/ppermute | solution.py:381
  28.1 28.2 %collective-permute-start.1 = (bf16[2048,128]{1,0:T(8,128)(2,1)S(1)}, bf16[2048,128]{1,0:T(8,128)(2,1)}, u32[]{:S(2)}, u32[]{:S(2)}) collective-permute-start(bf16[2048,128]{1,0:T(8,128)(2,1)S(1)} %bitcast.17), channel_id=1, source_target_pairs={{0,8},{8,0},{16,24},{24,16},{32,40},{40,32},{48,56},{56,48},{64,72... | collective-permute-start | bytes 1572872 | tf_op jit(solution)/shard_map/ppermute | solution.py:382
  42.0 1.3 %copy-start = (f32[4096,128]{1,0:T(8,128)}, f32[4096,128]{1,0:T(8,128)S(1)}, u32[]{:S(2)}) copy-start(f32[4096,128]{1,0:T(8,128)S(1)} %get-tuple-element.18.tail_ref) | copy-start | bytes 6291460
  80.2 42.8 %copy-start.1 = (f32[4096,128]{1,0:T(8,128)S(1)}, f32[4096,128]{1,0:T(8,128)}, u32[]{:S(2)}) copy-start(f32[4096,128]{1,0:T(8,128)} %copy-done) | copy-start | bytes 6291460

commit v6 on v5

--- a/solution.py
+++ b/solution.py
@@ -134,6 +134,15 @@
     sources = x_ref.shape[0]
     data = cap * per_row
     own_rows = k_ref.shape[0]
+    core = lax.axis_index("roll") & 1
+    kept = pl.ds(pl.multiple_of(core * own_rows, own_rows), own_rows)
+    other = pl.ds(pl.multiple_of((1 - core) * own_rows, own_rows), own_rows)
+    loads = [
+        pltpu.make_async_copy(ko_ref, key_ref.at[other, :], sems.at[1]),
+        pltpu.make_async_copy(vo_ref, wide_ref.at[other, pl.ds(0, 128)], sems.at[2]),
+    ]
+    for load in loads:
+        load.start()
     i = lax.broadcasted_iota(jnp.int32, (sources, sources), 0)
     j = lax.broadcasted_iota(jnp.int32, (sources, sources), 1)
     lower = (j <= i).astype(BF16)
@@ -163,17 +172,14 @@
     list_ref[...] = jnp.concatenate(lists + [end] + lists + [end], axis=0).astype(jnp.int32)
     copy = pltpu.make_async_copy(list_ref, where_ref, sems.at[0])
     copy.start()
-    core = lax.axis_index("roll") & 1
-    mine = pl.ds(pl.multiple_of(core * own_rows, own_rows), own_rows)
-    other = pl.ds(pl.multiple_of((1 - core) * own_rows, own_rows), own_rows)
-    key_ref[mine, :] = k_ref[...]
-    key_ref[other, :] = ko_ref[...]
-    wide_ref[mine, 0:128] = v_ref[...]
-    wide_ref[other, 0:128] = vo_ref[...]
+    key_ref[kept, :] = k_ref[...]
+    wide_ref[kept, 0:128] = v_ref[...]
     wide_ref[:, 128:256] = jnp.ones((2 * own_rows, 128), BF16)
     lse_ref[...] = jnp.zeros(lse_ref.shape, F32)
     copy.wait()
     found = where_ref[3, 0]
+    for load in loads:
+        load.wait()
     mask = lane_group_mask(per_row, 128)
     factor = scale * LOG2E
 
@@ -219,8 +225,10 @@
         return lax.fori_loop(0, lax.shift_right_logical(stop - begin + unit - 1, unit.bit_length() - 1), one, bounds)
 
     bounds = (jnp.ones((8, 128), F32), jnp.ones((8, 128), F32))
+    long = lax.shift_left(lax.shift_right_logical(found, 6), 6)
     most = lax.shift_left(lax.shift_right_logical(found + 8, 5), 5)
-    bounds = attend(32, 8, False, 0, most, bounds)
+    bounds = attend(64, 8, False, 0, long, bounds)
+    bounds = attend(32, 8, False, long, most, bounds)
     low, high = attend(16, 8, False, most, found, bounds)
     safe = (jnp.min(low) > 2.0**-70) & (jnp.max(high) < 2.0**100)
 
@@ -384,7 +392,7 @@
     answered = pl.pallas_call(
         functools.partial(prefix_kernel, cap, per_row, pref, scale),
         out_shape=pltpu.VMEM((owners, block, width), BF16),
-        in_specs=[vmem()] * 5,
+        in_specs=[vmem()] * 3 + [hbm()] * 2,
         out_specs=vmem(),
         scratch_shapes=[
             pltpu.VMEM((2 * groups * pref, width), BF16),
@@ -392,7 +400,7 @@
             pltpu.VMEM((8, 128), jnp.int32),
             pltpu.VMEM((owners * cap, 128), F32),
             pltpu.SMEM((8, 128), jnp.int32),
-            pltpu.SemaphoreType.DMA((1,)),
+            pltpu.SemaphoreType.DMA((3,)),
         ],
         compiler_params=params(24),
         cost_estimate=pl.CostEstimate(
@@ -400,7 +408,7 @@
             transcendentals=owners * cap * per_row * pref,
         ),
         name="prefix",
-    )(arrived, keys, values, keys_other, values_other)
+    )(arrived, in_vmem(keys), in_vmem(values), in_hbm(keys_other), in_hbm(values_other))
     back = lax.all_to_all(answered, "roll", split_axis=0, concat_axis=0, tiled=True)
 
     chunks = 4

time: 126 us -> 124 us (0.984)
  blocking collectives: 58.1 us -> 55.6 us
    all_to_all x1, blocking collectives: 42.8 us -> 40.2 us  [body(): lax.all_to_all(answered, 'roll', split_axis=0, concat_axis=0, tiled=True)]
where the time goes in v6:
time: 124 us; the launch traced here: 123 us
  blocking collectives  55.6 us (45%)
  Pallas kernels  42.1 us (34%)
  waiting for transfers between devices  13 us (10%)
  starting transfers between devices  9.9 us (8%)
  local copies, waits for them, and re-layouts  1.34 us (1%)
    all_to_all x1, blocking collectives, body(): lax.all_to_all(answered, 'roll', split_axis=0, concat_axis=0, tiled=True)  40.2 us
    pallas_call x1, Pallas kernels, body(): pl.pallas_call(functools.partial(prefix_kernel, cap, per_row, pref, scale...  24.1 us
    all_to_all x1, blocking collectives, body(): lax.all_to_all(jnp.broadcast_to(code, (lines, code.shape[1])), 'tp', spli...  15.3 us
    pallas_call x1, Pallas kernels, body(): pl.pallas_call(functools.partial(tail_kernel, steps, per_row, batch, scal...  13.6 us
    all_to_all x1, waiting for transfers between devices, body(): lax.all_to_all(sent, 'roll', split_axis=0, concat_axis=0, tiled=True)  13 us
    all_to_all x1, starting transfers between devices, body(): lax.all_to_all(sent, 'roll', split_axis=0, concat_axis=0, tiled=True)  9.31 us
  transfers between devices with their start and end apart: 3, of which 1 were waited for; matrix products, arithmetic and copies ran while one was open for 0% of the time, Pallas kernels for 11%

profile of v6, /device:TPU:1, one launch (start us, length us, event | category | flops | bytes accessed | tf_op | source)
XLA Modules:
  0.0 122.8 jit_solution(17745258376377170709)
XLA Ops:
  0.0 0.7 add_bitcast_fusion
  0.7 15.3 %all_to_all.18 = s32[8,1,16]{2,1,0:T(1,128)S(1)} all-to-all(s32[8,1,16]{2,1,0:T(1,128)S(1)} %broadcast_in_dim.2), channel_id=1, replica_groups=mesh['roll'=32,'tp'=8] {'tp'}, dimensions={0} | all-to-all | bytes 1024 | tf_op jit(solution)/shard_map/all_to_all | solution.py:329
  16.0 2.4 %pack.1 = (bf16[32,264,128]{2,1,0:T(8,128)(2,1)}, s32[1,128]{1,0:T(1,128)S(1)}) custom-call(s32[8,16]{1,0:T(8,128)S(1)} %bitcast.13, bf16[4096,128]{1,0:T(8,128)(2,1)} %bitcast.19), custom_call_target="tpu_custom_call" | custom-call | bytes 3145728 | tf_op jit(solution)/shard_map/pack/pallas_call | solution.py:335
  18.4 0.0 copy-start.4
  18.5 0.0 copy-start.5
  18.5 0.0 copy-start.2
  18.5 0.0 copy-start.3
  18.5 9.3 %all-to-all-start.1 = ((bf16[32,264,128]{2,1,0:T(8,128)(2,1)}), bf16[32,264,128]{2,1,0:T(8,128)(2,1)S(1)}, u32[]{:S(2)}, u32[]{:S(2)}) async-start(bf16[32,264,128]{2,1,0:T(8,128)(2,1)} %get-tuple-element.13), calls=%async_computation.1 | async-start | bytes 4325376 | tf_op jit(solution)/shard_map/all_to_all | solution.py:353
  27.8 0.0 copy-done.4
  27.8 0.3 collective-permute-start
  28.1 0.0 copy-done.5
  28.1 0.3 collective-permute-start.1
  28.4 0.0 copy-done.2
  28.4 0.0 copy-done.3
  28.4 13.6 %tail.1 = (f32[4096,128]{1,0:T(8,128)S(1)}, f32[128,128]{1,0:T(8,128)S(1)}) custom-call(s32[8,16]{1,0:T(8,128)S(1)} %bitcast.14, bf16[4096,128]{1,0:T(8,128)(2,1)} %bitcast.20, bf16[16384,128]{1,0:T(8,128)(2,1)} %bitcast.21, bf16[16384,128]{1,0:T(8,128)(2,1)} %bitcast.22, bf16[512,128]{1,0:T(8,128)(2,1)S(1)} %bitcast.11, bf16[512,128]{1,0:T(8,128)(2,1)S(1)} %bitcast.12), custom_call_target="tpu_custom_call" | custom-call | flops 268435456 | bytes 12582912 | tf_op jit(solution)/shard_map/tail/pallas_call | solution.py:357
  42.0 0.0 copy-start
  42.1 1.3 %copy-done = f32[4096,128]{1,0:T(8,128)} copy-done((f32[4096,128]{1,0:T(8,128)}, f32[4096,128]{1,0:T(8,128)S(1)}, u32[]{:S(2)}) %copy-start) | copy-done | bytes 2097176
  43.4 13.0 %all-to-all-done.1.x_ref = bf16[32,264,128]{2,1,0:T(8,128)(2,1)S(1)} async-done(((bf16[32,264,128]{2,1,0:T(8,128)(2,1)}), bf16[32,264,128]{2,1,0:T(8,128)(2,1)S(1)}, u32[]{:S(2)}, u32[]{:S(2)}) %all-to-all-start.1) | async-done | bytes 2162720 | tf_op jit(solution)/shard_map/all_to_all | solution.py:353
  56.4 0.0 collective-permute-done.ko_ref
  56.4 0.0 collective-permute-done.1.vo_ref
  56.4 24.1 %prefix.1 = bf16[32,264,128]{2,1,0:T(8,128)(2,1)S(1)} custom-call(bf16[32,264,128]{2,1,0:T(8,128)(2,1)S(1)} %all-to-all-done.1.x_ref, bf16[2048,128]{1,0:T(8,128)(2,1)S(1)} %bitcast.16, bf16[2048,128]{1,0:T(8,128)(2,1)S(1)} %bitcast.18, bf16[2048,128]{1,0:T(8,128)(2,1)} %collective-permute-done.ko_ref, bf16[2048,128]{1,0:T(8,128)(2,1)} %collective-permute-done.1.vo_ref), custom_call_target="tpu_custom_call" | custom-call | flops 4294967296 | bytes 6291456 | tf_op jit(solution)/shard_map/prefix/pallas_call | solution.py:392
  80.5 0.0 copy-start.1
  80.5 40.2 %all_to_all.19.x_ref = bf16[32,264,128]{2,1,0:T(8,128)(2,1)S(1)} all-to-all(bf16[32,264,128]{2,1,0:T(8,128)(2,1)S(1)} %prefix.1), channel_id=1, replica_groups=mesh['roll'=32,'tp'=8] {'roll'}, dimensions={0} | all-to-all | bytes 4325376 | tf_op jit(solution)/shard_map/all_to_all | solution.py:412
  120.7 0.0 copy-done.1
  120.7 2.1 %merge.1 = bf16[4096,128]{1,0:T(8,128)(2,1)} custom-call(s32[1,128]{1,0:T(1,128)S(1)} %get-tuple-element.12.place_ref, bf16[32,264,128]{2,1,0:T(8,128)(2,1)S(1)} %all_to_all.19.x_ref, f32[128,128]{1,0:T(8,128)S(1)} %get-tuple-element.17.lse_ref, f32[4096,128]{1,0:T(8,128)S(1)} %copy-done.1), custom_call_target="tpu_custom_call" | custom-call | bytes 6291456 | tf_op jit(solution)/shard_map/merge/pallas_call | solution.py:415
  (1 shorter events, 0.0 us)
Async XLA Ops:
  18.4 9.4 %copy-start.4 = (bf16[2,1,1024,128]{3,2,1,0:T(8,128)(2,1)S(1)}, bf16[2,1,1024,128]{3,2,1,0:T(8,128)(2,1)}, u32[]{:S(2)}) copy-start(bf16[2,1,1024,128]{3,2,1,0:T(8,128)(2,1)} %param.15) | copy-start | bytes 1572868
  18.5 9.7 %copy-start.5 = (bf16[2,1,1024,128]{3,2,1,0:T(8,128)(2,1)S(1)}, bf16[2,1,1024,128]{3,2,1,0:T(8,128)(2,1)}, u32[]{:S(2)}) copy-start(bf16[2,1,1024,128]{3,2,1,0:T(8,128)(2,1)} %param.16) | copy-start | bytes 1572868
  18.5 10.0 %copy-start.2 = (bf16[128,4,1,128]{3,1,2,0:T(4,128)(2,1)S(1)}, bf16[128,4,1,128]{3,1,2,0:T(4,128)(2,1)}, u32[]{:S(2)}) copy-start(bf16[128,4,1,128]{3,1,2,0:T(4,128)(2,1)} %param.11) | copy-start | bytes 393220
  18.5 9.9 %copy-start.3 = (bf16[128,4,1,128]{3,1,2,0:T(4,128)(2,1)S(1)}, bf16[128,4,1,128]{3,1,2,0:T(4,128)(2,1)}, u32[]{:S(2)}) copy-start(bf16[128,4,1,128]{3,1,2,0:T(4,128)(2,1)} %param.12) | copy-start | bytes 393220
  18.5 37.9 %all-to-all-start.1 = ((bf16[32,264,128]{2,1,0:T(8,128)(2,1)}), bf16[32,264,128]{2,1,0:T(8,128)(2,1)S(1)}, u32[]{:S(2)}, u32[]{:S(2)}) async-start(bf16[32,264,128]{2,1,0:T(8,128)(2,1)} %get-tuple-element.13), calls=%async_computation.1 | async-start | bytes 4325376 | tf_op jit(solution)/shard_map/all_to_all | solution.py:353
  27.8 28.6 %collective-permute-start = (bf16[2048,128]{1,0:T(8,128)(2,1)S(1)}, bf16[2048,128]{1,0:T(8,128)(2,1)}, u32[]{:S(2)}, u32[]{:S(2)}) collective-permute-start(bf16[2048,128]{1,0:T(8,128)(2,1)S(1)} %bitcast.15), channel_id=1, source_target_pairs={{0,8},{8,0},{16,24},{24,16},{32,40},{40,32},{48,56},{56,48},{64,72... | collective-permute-start | bytes 1572872 | tf_op jit(solution)/shard_map/ppermute | solution.py:389
  28.1 28.2 %collective-permute-start.1 = (bf16[2048,128]{1,0:T(8,128)(2,1)S(1)}, bf16[2048,128]{1,0:T(8,128)(2,1)}, u32[]{:S(2)}, u32[]{:S(2)}) collective-permute-start(bf16[2048,128]{1,0:T(8,128)(2,1)S(1)} %bitcast.17), channel_id=1, source_target_pairs={{0,8},{8,0},{16,24},{24,16},{32,40},{40,32},{48,56},{56,48},{64,72... | collective-permute-start | bytes 1572872 | tf_op jit(solution)/shard_map/ppermute | solution.py:390
  42.0 1.3 %copy-start = (f32[4096,128]{1,0:T(8,128)}, f32[4096,128]{1,0:T(8,128)S(1)}, u32[]{:S(2)}) copy-start(f32[4096,128]{1,0:T(8,128)S(1)} %get-tuple-element.18.tail_ref) | copy-start | bytes 6291460
  80.5 40.2 %copy-start.1 = (f32[4096,128]{1,0:T(8,128)S(1)}, f32[4096,128]{1,0:T(8,128)}, u32[]{:S(2)}) copy-start(f32[4096,128]{1,0:T(8,128)} %copy-done) | copy-start | bytes 6291460

commit v7 on v6

--- a/solution.py
+++ b/solution.py
@@ -12,7 +12,8 @@
 MIB = 1 << 20
 F32 = jnp.float32
 BF16 = jnp.bfloat16
-EXTRA = 8
+EXTRA = 16
+BACK = 8
 
 
 def lane_group_mask(per_row, width):
@@ -61,7 +62,7 @@
     counts = jnp.dot(named.astype(BF16), jnp.ones((rows, 128), BF16), preferred_element_type=F32).astype(BF16)
     ii = lax.broadcasted_iota(jnp.int32, (owners * EXTRA, 4 * owners), 0)
     kk = lax.broadcasted_iota(jnp.int32, (owners * EXTRA, 4 * owners), 1)
-    repeat = (lax.shift_right_logical(ii, 1) == kk).astype(BF16)
+    repeat = (lax.shift_right_logical(ii, 2) == kk).astype(BF16)
     extra_ref[...] = jnp.dot(repeat, counts, preferred_element_type=F32).astype(BF16).reshape(owners, EXTRA, 128)
     more = pltpu.make_async_copy(extra_ref, out_ref.at[:, pl.ds(cap * per_row, EXTRA), :], sems.at[2])
     more.start()
@@ -153,7 +154,7 @@
     end = jnp.zeros((1, 128), F32)
     tables = []
     for g in range(4):
-        count = jnp.concatenate([tile[2 * g:2 * g + 1, :] for tile in tiles], axis=0)
+        count = jnp.concatenate([tile[4 * g:4 * g + 1, :] for tile in tiles], axis=0)
         ends = jnp.dot(lower, count.astype(BF16), preferred_element_type=F32)
         total = ends[sources - 1:sources, :]
         tables.append((end, total, ends - count, ends, source * cap + fore))
@@ -244,7 +245,7 @@
         low_part = rest - mid_part
         lanes = lax.broadcasted_iota(jnp.int32, full.shape, 1)
         sent = jnp.where(lanes < per_row, high_part, jnp.where(lanes < 2 * per_row, mid_part, low_part))
-        out_ref[s, data:data + EXTRA, :] = sent.astype(BF16)
+        out_ref[s, data:data + BACK, :] = sent.astype(BF16)
 
 
 def merge_kernel(cap, per_row, chunks, place_ref, x_ref, lse_ref, tail_ref, out_ref, sent_ref, weight_ref, done_ref, sems):
@@ -259,7 +260,7 @@
 
     stores = [pltpu.make_async_copy(piece(done_ref, c), piece(out_ref, c), sems.at[c]) for c in range(chunks)]
     for o in range(owners):
-        sent_ref[o * cap:(o + 1) * cap, :] = x_ref[o, data:data + EXTRA, :].astype(F32)[0:cap, :]
+        sent_ref[o * cap:(o + 1) * cap, :] = x_ref[o, data:data + BACK, :].astype(F32)
     mask = lane_group_mask(per_row, 128)
     lane = lax.broadcasted_iota(jnp.int32, (batch, 128), 1)
     ones = jnp.ones((128, 128), BF16)
@@ -391,7 +392,7 @@
     arrived, tail_out, tail_lse = lax.optimization_barrier((arrived, tail_out, tail_lse))
     answered = pl.pallas_call(
         functools.partial(prefix_kernel, cap, per_row, pref, scale),
-        out_shape=pltpu.VMEM((owners, block, width), BF16),
+        out_shape=pltpu.VMEM((owners, cap * per_row + BACK, width), BF16),
         in_specs=[vmem()] * 3 + [hbm()] * 2,
         out_specs=vmem(),
         scratch_shapes=[

time: 124 us -> 127 us (1.024); the launches traced: 123 us -> 127 us
  Pallas kernels: 42.1 us -> 50.2 us
  blocking collectives: 55.6 us -> 51.3 us
    pallas_call x1, Pallas kernels: 24.1 us -> 32.2 us  [body(): pl.pallas_call(functools.partial(prefix_kernel, cap, per_row, pref, scale...]
    all_to_all x1, blocking collectives: 40.2 us -> 35.9 us  [body(): lax.all_to_all(answered, 'roll', split_axis=0, concat_axis=0, tiled=True)]
where the time goes in v7:
time: 127 us
  blocking collectives  51.3 us (40%)
  Pallas kernels  50.2 us (40%)
  waiting for transfers between devices  13.7 us (11%)
  starting transfers between devices  9.91 us (8%)
  local copies, waits for them, and re-layouts  1.34 us (1%)
    all_to_all x1, blocking collectives, body(): lax.all_to_all(answered, 'roll', split_axis=0, concat_axis=0, tiled=True)  35.9 us
    pallas_call x1, Pallas kernels, body(): pl.pallas_call(functools.partial(prefix_kernel, cap, per_row, pref, scale...  32.2 us
    all_to_all x1, blocking collectives, body(): lax.all_to_all(jnp.broadcast_to(code, (lines, code.shape[1])), 'tp', spli...  15.3 us
    all_to_all x1, waiting for transfers between devices, body(): lax.all_to_all(sent, 'roll', split_axis=0, concat_axis=0, tiled=True)  13.7 us
    pallas_call x1, Pallas kernels, body(): pl.pallas_call(functools.partial(tail_kernel, steps, per_row, batch, scal...  13.6 us
    all_to_all x1, starting transfers between devices, body(): lax.all_to_all(sent, 'roll', split_axis=0, concat_axis=0, tiled=True)  9.31 us
  transfers between devices with their start and end apart: 3, of which 1 were waited for; matrix products, arithmetic and copies ran while one was open for 0% of the time, Pallas kernels for 11%

profile of v7, /device:TPU:1, one launch (start us, length us, event | category | flops | bytes accessed | tf_op | source)
XLA Modules:
  0.0 127.3 jit_solution(11356649285784263012)
XLA Ops:
  0.0 0.7 add_bitcast_fusion
  0.7 15.3 %all_to_all.18 = s32[8,1,16]{2,1,0:T(1,128)S(1)} all-to-all(s32[8,1,16]{2,1,0:T(1,128)S(1)} %broadcast_in_dim.2), channel_id=1, replica_groups=mesh['roll'=32,'tp'=8] {'tp'}, dimensions={0} | all-to-all | bytes 1024 | tf_op jit(solution)/shard_map/all_to_all | solution.py:330
  16.0 2.4 %pack.1 = (bf16[32,272,128]{2,1,0:T(8,128)(2,1)}, s32[1,128]{1,0:T(1,128)S(1)}) custom-call(s32[8,16]{1,0:T(8,128)S(1)} %bitcast.13, bf16[4096,128]{1,0:T(8,128)(2,1)} %bitcast.17), custom_call_target="tpu_custom_call" | custom-call | bytes 3145728 | tf_op jit(solution)/shard_map/pack/pallas_call | solution.py:336
  18.4 0.0 copy-start.4
  18.5 0.0 copy-start.2
  18.5 0.0 copy-start.3
  18.5 9.3 %all-to-all-start.1 = ((bf16[32,272,128]{2,1,0:T(8,128)(2,1)}), bf16[32,272,128]{2,1,0:T(8,128)(2,1)S(1)}, u32[]{:S(2)}, u32[]{:S(2)}) async-start(bf16[32,272,128]{2,1,0:T(8,128)(2,1)} %get-tuple-element.13), calls=%async_computation.1 | async-start | bytes 4456448 | tf_op jit(solution)/shard_map/all_to_all | solution.py:354
  27.8 0.0 copy-done.4
  27.8 0.3 collective-permute-start
  28.1 0.3 collective-permute-start.1
  28.4 0.0 copy-done.2
  28.4 0.0 copy-done.3
  28.4 13.6 %tail.1 = (f32[4096,128]{1,0:T(8,128)S(1)}, f32[128,128]{1,0:T(8,128)S(1)}) custom-call(s32[8,16]{1,0:T(8,128)S(1)} %bitcast.14, bf16[4096,128]{1,0:T(8,128)(2,1)} %bitcast.18, bf16[16384,128]{1,0:T(8,128)(2,1)} %bitcast.19, bf16[16384,128]{1,0:T(8,128)(2,1)} %bitcast.20, bf16[512,128]{1,0:T(8,128)(2,1)S(1)} %bitcast.11, bf16[512,128]{1,0:T(8,128)(2,1)S(1)} %bitcast.12), custom_call_target="tpu_custom_call" | custom-call | flops 268435456 | bytes 12582912 | tf_op jit(solution)/shard_map/tail/pallas_call | solution.py:358
  42.0 0.0 copy-start
  42.0 1.3 %copy-done = f32[4096,128]{1,0:T(8,128)} copy-done((f32[4096,128]{1,0:T(8,128)}, f32[4096,128]{1,0:T(8,128)S(1)}, u32[]{:S(2)}) %copy-start) | copy-done | bytes 2097176
  43.4 13.7 %all-to-all-done.1.x_ref = bf16[32,272,128]{2,1,0:T(8,128)(2,1)S(1)} async-done(((bf16[32,272,128]{2,1,0:T(8,128)(2,1)}), bf16[32,272,128]{2,1,0:T(8,128)(2,1)S(1)}, u32[]{:S(2)}, u32[]{:S(2)}) %all-to-all-start.1) | async-done | bytes 2228256 | tf_op jit(solution)/shard_map/all_to_all | solution.py:354
  57.1 0.0 collective-permute-done.ko_ref
  57.1 0.0 collective-permute-done.1.vo_ref
  57.1 32.2 %prefix.1 = bf16[32,264,128]{2,1,0:T(8,128)(2,1)S(1)} custom-call(bf16[32,272,128]{2,1,0:T(8,128)(2,1)S(1)} %all-to-all-done.1.x_ref, bf16[2048,128]{1,0:T(8,128)(2,1)S(1)} %bitcast.16, bf16[2048,128]{1,0:T(8,128)(2,1)} %bitcast.8.v_ref, bf16[2048,128]{1,0:T(8,128)(2,1)} %collective-permute-done.ko_ref, bf16[2048,128]{1,0:T(8,128)(2,1)} %collective-permute-done.1.vo_ref), custom_call_target="tpu_custom_call" | custom-call | flops 4294967296 | bytes 6291456 | tf_op jit(solution)/shard_map/prefix/pallas_call | solution.py:393
  89.2 0.0 copy-start.1
  89.2 35.9 %all_to_all.19.x_ref = bf16[32,264,128]{2,1,0:T(8,128)(2,1)S(1)} all-to-all(bf16[32,264,128]{2,1,0:T(8,128)(2,1)S(1)} %prefix.1), channel_id=1, replica_groups=mesh['roll'=32,'tp'=8] {'roll'}, dimensions={0} | all-to-all | bytes 4325376 | tf_op jit(solution)/shard_map/all_to_all | solution.py:413
  125.2 0.0 copy-done.1
  125.2 2.1 %merge.1 = bf16[4096,128]{1,0:T(8,128)(2,1)} custom-call(s32[1,128]{1,0:T(1,128)S(1)} %get-tuple-element.12.place_ref, bf16[32,264,128]{2,1,0:T(8,128)(2,1)S(1)} %all_to_all.19.x_ref, f32[128,128]{1,0:T(8,128)S(1)} %get-tuple-element.17.lse_ref, f32[4096,128]{1,0:T(8,128)S(1)} %copy-done.1), custom_call_target="tpu_custom_call" | custom-call | bytes 6291456 | tf_op jit(solution)/shard_map/merge/pallas_call | solution.py:416
  (1 shorter events, 0.0 us)
Async XLA Ops:
  18.4 9.4 %copy-start.4 = (bf16[2,1,1024,128]{3,2,1,0:T(8,128)(2,1)S(1)}, bf16[2,1,1024,128]{3,2,1,0:T(8,128)(2,1)}, u32[]{:S(2)}) copy-start(bf16[2,1,1024,128]{3,2,1,0:T(8,128)(2,1)} %param.15) | copy-start | bytes 1572868
  18.5 10.0 %copy-start.2 = (bf16[128,4,1,128]{3,1,2,0:T(4,128)(2,1)S(1)}, bf16[128,4,1,128]{3,1,2,0:T(4,128)(2,1)}, u32[]{:S(2)}) copy-start(bf16[128,4,1,128]{3,1,2,0:T(4,128)(2,1)} %param.11) | copy-start | bytes 393220
  18.5 9.9 %copy-start.3 = (bf16[128,4,1,128]{3,1,2,0:T(4,128)(2,1)S(1)}, bf16[128,4,1,128]{3,1,2,0:T(4,128)(2,1)}, u32[]{:S(2)}) copy-start(bf16[128,4,1,128]{3,1,2,0:T(4,128)(2,1)} %param.12) | copy-start | bytes 393220
  18.5 38.6 %all-to-all-start.1 = ((bf16[32,272,128]{2,1,0:T(8,128)(2,1)}), bf16[32,272,128]{2,1,0:T(8,128)(2,1)S(1)}, u32[]{:S(2)}, u32[]{:S(2)}) async-start(bf16[32,272,128]{2,1,0:T(8,128)(2,1)} %get-tuple-element.13), calls=%async_computation.1 | async-start | bytes 4456448 | tf_op jit(solution)/shard_map/all_to_all | solution.py:354
  27.8 29.3 %collective-permute-start = (bf16[2048,128]{1,0:T(8,128)(2,1)S(1)}, bf16[2048,128]{1,0:T(8,128)(2,1)}, u32[]{:S(2)}, u32[]{:S(2)}) collective-permute-start(bf16[2048,128]{1,0:T(8,128)(2,1)S(1)} %bitcast.15), channel_id=1, source_target_pairs={{0,8},{8,0},{16,24},{24,16},{32,40},{40,32},{48,56},{56,48},{64,72... | collective-permute-start | bytes 1572872 | tf_op jit(solution)/shard_map/ppermute | solution.py:390
  28.1 28.9 %collective-permute-start.1 = (bf16[2048,128]{1,0:T(8,128)(2,1)}, bf16[2048,128]{1,0:T(8,128)(2,1)}, u32[]{:S(2)}, u32[]{:S(2)}) collective-permute-start(bf16[2048,128]{1,0:T(8,128)(2,1)} %bitcast.8.v_ref), channel_id=1, source_target_pairs={{0,8},{8,0},{16,24},{24,16},{32,40},{40,32},{48,56},{56,48},{64,72... | collective-permute-start | bytes 1572872 | tf_op jit(solution)/shard_map/ppermute | solution.py:391
  42.0 1.3 %copy-start = (f32[4096,128]{1,0:T(8,128)}, f32[4096,128]{1,0:T(8,128)S(1)}, u32[]{:S(2)}) copy-start(f32[4096,128]{1,0:T(8,128)S(1)} %get-tuple-element.18.tail_ref) | copy-start | bytes 6291460
  89.2 36.0 %copy-start.1 = (f32[4096,128]{1,0:T(8,128)S(1)}, f32[4096,128]{1,0:T(8,128)}, u32[]{:S(2)}) copy-start(f32[4096,128]{1,0:T(8,128)} %copy-done) | copy-start | bytes 6291460

commit v8 on v6

--- a/solution.py
+++ b/solution.py
@@ -227,7 +227,9 @@
     bounds = (jnp.ones((8, 128), F32), jnp.ones((8, 128), F32))
     long = lax.shift_left(lax.shift_right_logical(found, 6), 6)
     most = lax.shift_left(lax.shift_right_logical(found + 8, 5), 5)
-    bounds = attend(64, 8, False, 0, long, bounds)
+    longest = lax.shift_left(lax.shift_right_logical(found, 7), 7)
+    bounds = attend(128, 8, False, 0, longest, bounds)
+    bounds = attend(64, 8, False, longest, long, bounds)
     bounds = attend(32, 8, False, long, most, bounds)
     low, high = attend(16, 8, False, most, found, bounds)
     safe = (jnp.min(low) > 2.0**-70) & (jnp.max(high) < 2.0**100)

time: 124 us -> 123 us (level)
  Pallas kernels: 42.1 us -> 40.5 us
  blocking collectives: 55.6 us -> 57.1 us
    pallas_call x1, Pallas kernels: 24.1 us -> 22.4 us  [body(): pl.pallas_call(functools.partial(prefix_kernel, cap, per_row, pref, scale...]
    all_to_all x1, blocking collectives: 40.2 us -> 41.7 us  [body(): lax.all_to_all(answered, 'roll', split_axis=0, concat_axis=0, tiled=True)]
where the time goes in v8:
time: 123 us
  blocking collectives  57.1 us (46%)
  Pallas kernels  40.5 us (33%)
  waiting for transfers between devices  13 us (11%)
  starting transfers between devices  9.93 us (8%)
  local copies, waits for them, and re-layouts  1.34 us (1%)
    all_to_all x1, blocking collectives, body(): lax.all_to_all(answered, 'roll', split_axis=0, concat_axis=0, tiled=True)  41.7 us
    pallas_call x1, Pallas kernels, body(): pl.pallas_call(functools.partial(prefix_kernel, cap, per_row, pref, scale...  22.4 us
    all_to_all x1, blocking collectives, body(): lax.all_to_all(jnp.broadcast_to(code, (lines, code.shape[1])), 'tp', spli...  15.3 us
    pallas_call x1, Pallas kernels, body(): pl.pallas_call(functools.partial(tail_kernel, steps, per_row, batch, scal...  13.6 us
    all_to_all x1, waiting for transfers between devices, body(): lax.all_to_all(sent, 'roll', split_axis=0, concat_axis=0, tiled=True)  13 us
    all_to_all x1, starting transfers between devices, body(): lax.all_to_all(sent, 'roll', split_axis=0, concat_axis=0, tiled=True)  9.33 us
  transfers between devices with their start and end apart: 3, of which 1 were waited for; matrix products, arithmetic and copies ran while one was open for 0% of the time, Pallas kernels for 11%

profile of v8, /device:TPU:1, one launch (start us, length us, event | category | flops | bytes accessed | tf_op | source)
XLA Modules:
  0.0 122.6 jit_solution(11552965651067195427)
XLA Ops:
  0.0 0.7 add_bitcast_fusion
  0.7 15.3 %all_to_all.18 = s32[8,1,16]{2,1,0:T(1,128)S(1)} all-to-all(s32[8,1,16]{2,1,0:T(1,128)S(1)} %broadcast_in_dim.2), channel_id=1, replica_groups=mesh['roll'=32,'tp'=8] {'tp'}, dimensions={0} | all-to-all | bytes 1024 | tf_op jit(solution)/shard_map/all_to_all | solution.py:331
  16.0 2.4 %pack.1 = (bf16[32,264,128]{2,1,0:T(8,128)(2,1)}, s32[1,128]{1,0:T(1,128)S(1)}) custom-call(s32[8,16]{1,0:T(8,128)S(1)} %bitcast.13, bf16[4096,128]{1,0:T(8,128)(2,1)} %bitcast.19), custom_call_target="tpu_custom_call" | custom-call | bytes 3145728 | tf_op jit(solution)/shard_map/pack/pallas_call | solution.py:337
  18.4 0.0 copy-start.4
  18.4 0.0 copy-start.5
  18.4 0.0 copy-start.2
  18.5 0.0 copy-start.3
  18.5 9.3 %all-to-all-start.1 = ((bf16[32,264,128]{2,1,0:T(8,128)(2,1)}), bf16[32,264,128]{2,1,0:T(8,128)(2,1)S(1)}, u32[]{:S(2)}, u32[]{:S(2)}) async-start(bf16[32,264,128]{2,1,0:T(8,128)(2,1)} %get-tuple-element.13), calls=%async_computation.1 | async-start | bytes 4325376 | tf_op jit(solution)/shard_map/all_to_all | solution.py:355
  27.8 0.0 copy-done.4
  27.8 0.3 collective-permute-start
  28.1 0.0 copy-done.5
  28.1 0.3 collective-permute-start.1
  28.4 0.0 copy-done.2
  28.4 0.0 copy-done.3
  28.4 13.6 %tail.1 = (f32[4096,128]{1,0:T(8,128)S(1)}, f32[128,128]{1,0:T(8,128)S(1)}) custom-call(s32[8,16]{1,0:T(8,128)S(1)} %bitcast.14, bf16[4096,128]{1,0:T(8,128)(2,1)} %bitcast.20, bf16[16384,128]{1,0:T(8,128)(2,1)} %bitcast.21, bf16[16384,128]{1,0:T(8,128)(2,1)} %bitcast.22, bf16[512,128]{1,0:T(8,128)(2,1)S(1)} %bitcast.11, bf16[512,128]{1,0:T(8,128)(2,1)S(1)} %bitcast.12), custom_call_target="tpu_custom_call" | custom-call | flops 268435456 | bytes 12582912 | tf_op jit(solution)/shard_map/tail/pallas_call | solution.py:359
  42.0 0.0 copy-start
  42.0 1.3 %copy-done = f32[4096,128]{1,0:T(8,128)} copy-done((f32[4096,128]{1,0:T(8,128)}, f32[4096,128]{1,0:T(8,128)S(1)}, u32[]{:S(2)}) %copy-start) | copy-done | bytes 2097176
  43.4 13.0 %all-to-all-done.1.x_ref = bf16[32,264,128]{2,1,0:T(8,128)(2,1)S(1)} async-done(((bf16[32,264,128]{2,1,0:T(8,128)(2,1)}), bf16[32,264,128]{2,1,0:T(8,128)(2,1)S(1)}, u32[]{:S(2)}, u32[]{:S(2)}) %all-to-all-start.1) | async-done | bytes 2162720 | tf_op jit(solution)/shard_map/all_to_all | solution.py:355
  56.4 0.0 collective-permute-done.ko_ref
  56.4 0.0 collective-permute-done.1.vo_ref
  56.4 22.4 %prefix.1 = bf16[32,264,128]{2,1,0:T(8,128)(2,1)S(1)} custom-call(bf16[32,264,128]{2,1,0:T(8,128)(2,1)S(1)} %all-to-all-done.1.x_ref, bf16[2048,128]{1,0:T(8,128)(2,1)S(1)} %bitcast.16, bf16[2048,128]{1,0:T(8,128)(2,1)S(1)} %bitcast.18, bf16[2048,128]{1,0:T(8,128)(2,1)} %collective-permute-done.ko_ref, bf16[2048,128]{1,0:T(8,128)(2,1)} %collective-permute-done.1.vo_ref), custom_call_target="tpu_custom_call" | custom-call | flops 4294967296 | bytes 6291456 | tf_op jit(solution)/shard_map/prefix/pallas_call | solution.py:394
  78.8 0.0 copy-start.1
  78.8 41.7 %all_to_all.19.x_ref = bf16[32,264,128]{2,1,0:T(8,128)(2,1)S(1)} all-to-all(bf16[32,264,128]{2,1,0:T(8,128)(2,1)S(1)} %prefix.1), channel_id=1, replica_groups=mesh['roll'=32,'tp'=8] {'roll'}, dimensions={0} | all-to-all | bytes 4325376 | tf_op jit(solution)/shard_map/all_to_all | solution.py:414
  120.5 0.0 copy-done.1
  120.5 2.1 %merge.1 = bf16[4096,128]{1,0:T(8,128)(2,1)} custom-call(s32[1,128]{1,0:T(1,128)S(1)} %get-tuple-element.12.place_ref, bf16[32,264,128]{2,1,0:T(8,128)(2,1)S(1)} %all_to_all.19.x_ref, f32[128,128]{1,0:T(8,128)S(1)} %get-tuple-element.17.lse_ref, f32[4096,128]{1,0:T(8,128)S(1)} %copy-done.1), custom_call_target="tpu_custom_call" | custom-call | bytes 6291456 | tf_op jit(solution)/shard_map/merge/pallas_call | solution.py:417
  (1 shorter events, 0.0 us)
Async XLA Ops:
  18.4 9.4 %copy-start.4 = (bf16[2,1,1024,128]{3,2,1,0:T(8,128)(2,1)S(1)}, bf16[2,1,1024,128]{3,2,1,0:T(8,128)(2,1)}, u32[]{:S(2)}) copy-start(bf16[2,1,1024,128]{3,2,1,0:T(8,128)(2,1)} %param.15) | copy-start | bytes 1572868
  18.4 9.7 %copy-start.5 = (bf16[2,1,1024,128]{3,2,1,0:T(8,128)(2,1)S(1)}, bf16[2,1,1024,128]{3,2,1,0:T(8,128)(2,1)}, u32[]{:S(2)}) copy-start(bf16[2,1,1024,128]{3,2,1,0:T(8,128)(2,1)} %param.16) | copy-start | bytes 1572868
  18.4 10.0 %copy-start.2 = (bf16[128,4,1,128]{3,1,2,0:T(4,128)(2,1)S(1)}, bf16[128,4,1,128]{3,1,2,0:T(4,128)(2,1)}, u32[]{:S(2)}) copy-start(bf16[128,4,1,128]{3,1,2,0:T(4,128)(2,1)} %param.11) | copy-start | bytes 393220
  18.5 10.0 %copy-start.3 = (bf16[128,4,1,128]{3,1,2,0:T(4,128)(2,1)S(1)}, bf16[128,4,1,128]{3,1,2,0:T(4,128)(2,1)}, u32[]{:S(2)}) copy-start(bf16[128,4,1,128]{3,1,2,0:T(4,128)(2,1)} %param.12) | copy-start | bytes 393220
  18.5 37.9 %all-to-all-start.1 = ((bf16[32,264,128]{2,1,0:T(8,128)(2,1)}), bf16[32,264,128]{2,1,0:T(8,128)(2,1)S(1)}, u32[]{:S(2)}, u32[]{:S(2)}) async-start(bf16[32,264,128]{2,1,0:T(8,128)(2,1)} %get-tuple-element.13), calls=%async_computation.1 | async-start | bytes 4325376 | tf_op jit(solution)/shard_map/all_to_all | solution.py:355
  27.8 28.6 %collective-permute-start = (bf16[2048,128]{1,0:T(8,128)(2,1)S(1)}, bf16[2048,128]{1,0:T(8,128)(2,1)}, u32[]{:S(2)}, u32[]{:S(2)}) collective-permute-start(bf16[2048,128]{1,0:T(8,128)(2,1)S(1)} %bitcast.15), channel_id=1, source_target_pairs={{0,8},{8,0},{16,24},{24,16},{32,40},{40,32},{48,56},{56,48},{64,72... | collective-permute-start | bytes 1572872 | tf_op jit(solution)/shard_map/ppermute | solution.py:391
  28.1 28.2 %collective-permute-start.1 = (bf16[2048,128]{1,0:T(8,128)(2,1)S(1)}, bf16[2048,128]{1,0:T(8,128)(2,1)}, u32[]{:S(2)}, u32[]{:S(2)}) collective-permute-start(bf16[2048,128]{1,0:T(8,128)(2,1)S(1)} %bitcast.17), channel_id=1, source_target_pairs={{0,8},{8,0},{16,24},{24,16},{32,40},{40,32},{48,56},{56,48},{64,72... | collective-permute-start | bytes 1572872 | tf_op jit(solution)/shard_map/ppermute | solution.py:392
  42.0 1.3 %copy-start = (f32[4096,128]{1,0:T(8,128)}, f32[4096,128]{1,0:T(8,128)S(1)}, u32[]{:S(2)}) copy-start(f32[4096,128]{1,0:T(8,128)S(1)} %get-tuple-element.18.tail_ref) | copy-start | bytes 6291460
  78.8 41.7 %copy-start.1 = (f32[4096,128]{1,0:T(8,128)S(1)}, f32[4096,128]{1,0:T(8,128)}, u32[]{:S(2)}) copy-start(f32[4096,128]{1,0:T(8,128)} %copy-done) | copy-start | bytes 6291460
